TPU v7x, 32 devices: a whole 2x2x4 slice. The times are simulated.
32 devices in a mesh: expert: 8 (over y, x, core), tensor: 4 (over z).
Axes of the slice: x: 2, y: 2, z: 4, core: 2. Of those that a mesh axis runs over, the one named last changes fastest.
Arguments:
- tokens: bfloat16 [4096, 1024], P('expert'), may hold values from -6 to 6
- norm1_gain: float32 [1024], replicated, may hold values from 0.5 to 1.5
- w_query: bfloat16 [1024, 1024], P(None, 'tensor'), may hold values from -0.1875 to 0.1875
- key_projection_weight: bfloat16 [1024, 512], P(None, 'tensor'), may hold values from -0.1875 to 0.1875
- value_projection_weight: bfloat16 [1024, 512], P(None, 'tensor'), may hold values from -0.1875 to 0.1875
- w_output: bfloat16 [1024, 1024], P('tensor'), may hold values from -1.5 to 1.5
- norm2_gain: float32 [1024], replicated, may hold values from 0.5 to 1.5
- w_router: bfloat16 [1024, 32], replicated, may hold values from -0.09375 to 0.09375
- expert_gate_weight: bfloat16 [32, 1024, 512], P('expert', None, 'tensor'), may hold values from -0.1875 to 0.1875
- expert_up_weight: bfloat16 [32, 1024, 512], P('expert', None, 'tensor'), may hold values from -0.1875 to 0.1875
- expert_down_weight: bfloat16 [32, 512, 1024], P('expert', 'tensor'), may hold values from -0.75 to 0.75
- expert_ids: int32 [4096, 8], P('expert'), may hold values from 0 to 31, all different within a row; in each aligned block of 512 rows (0 to 511, 512 to 1023, ...) at most 160 rows name the same one
- cotangent: bfloat16 [4096, 1024], P('expert'), may hold values from -6 to 6
Outputs:
- mixed: bfloat16 [4096, 1024], P('expert', 'tensor')
- grad_input: float32 [4096, 1024], P('expert')
- grad_norm1: float32 [1024], replicated
- grad_query: float32 [1024, 1024], P(None, 'tensor')
- grad_key: float32 [1024, 512], P(None, 'tensor')
- grad_value: float32 [1024, 512], P(None, 'tensor')
- grad_output: float32 [1024, 1024], P('tensor')
- grad_norm2: float32 [1024], replicated
- grad_router: float32 [1024, 32], replicated
- grad_gate: float32 [32, 1024, 512], P('expert', None, 'tensor')
- up_weight_gradient: float32 [32, 1024, 512], P('expert', None, 'tensor')
- grad_down: float32 [32, 512, 1024], P('expert', 'tensor')
Inputs may be any that keep to these rules, and one draw needn't show every extreme that they name: `expert_ids`: within the rows of one index of expert (512 tokens), no expert is named more than 160 times, a bound that some block reaches.
All inputs are finite; a program needn't handle non-finite values.
Results may differ from a plain program's by a relative error of at most 0.023.
Values may be sent and summed in bfloat16 or wider, within the bound.
No kernel may reach another device: no remote copies, remote signals or barrier semaphores. Data moves between devices by JAX's collectives and lax.ppermute only.
A program may use at most 192 MiB of HBM per device.

v0:
```python
import math

import jax
import jax.numpy as jnp
from jax import lax
from jax.sharding import PartitionSpec as P

HEAD_DIMENSION = 64
SEQ_LEN = 512
CAP = 160


EPS = 1e-06
SCALE = 0.125
NEGATIVE = -1e30
THETA = 10000.0


def tables(tok_count):
    half = HEAD_DIMENSION // 2
    freq = jnp.exp(-math.log(THETA) * jnp.arange(half, dtype=jnp.float32) / half)
    places = (jnp.arange(tok_count) % SEQ_LEN).astype(jnp.float32)
    angle = places[:, None] * freq[None, :]
    return (jnp.cos(angle)[:, None, :], jnp.sin(angle)[:, None, :])


def rotate(field, cosine, sine_table, factor):
    half = HEAD_DIMENSION // 2
    first = field[..., :half]
    second = field[..., half:]
    return jnp.concatenate(
        [
            first * cosine - factor * second * sine_table,
            second * cosine + factor * first * sine_table,
        ],
        axis=-1,
    )


def causal_mask():
    places = jnp.arange(SEQ_LEN)
    return places[:, None] >= places[None, :]


def attend_forward(parts):
    query_rows, rotated_keys, value_rows = parts
    scores = (
        jnp.einsum("lkgd,mkd->kglm", query_rows, rotated_keys, preferred_element_type=jnp.float32)
        * SCALE
    )
    scores = jnp.where(causal_mask(), scores, NEGATIVE)
    highest = jnp.max(scores, axis=-1, keepdims=True)
    expanded = jnp.exp(scores - highest)
    summed = jnp.sum(expanded, axis=-1, keepdims=True)
    probability = (expanded / summed).astype(jnp.bfloat16)
    heads_out = jnp.einsum(
        "kglm,mkd->lkgd", probability, value_rows, preferred_element_type=jnp.float32
    )
    return (heads_out.astype(jnp.bfloat16), (highest + jnp.log(summed))[..., 0])


def attend_backward(parts):
    query_rows, rotated_keys, value_rows, grad_heads, log_total = parts
    scores = (
        jnp.einsum("lkgd,mkd->kglm", query_rows, rotated_keys, preferred_element_type=jnp.float32)
        * SCALE
    )
    probability = jnp.where(causal_mask(), jnp.exp(scores - log_total[..., None]), 0.0)
    prob_low = probability.astype(jnp.bfloat16)
    grad_values = jnp.einsum(
        "kglm,lkgd->mkd", prob_low, grad_heads, preferred_element_type=jnp.float32
    )
    grad_prob = jnp.einsum(
        "lkgd,mkd->kglm", grad_heads, value_rows, preferred_element_type=jnp.float32
    )
    row_delta = jnp.sum(probability * grad_prob, axis=-1, keepdims=True)
    grad_scores = (probability * (grad_prob - row_delta)).astype(jnp.bfloat16)
    grad_queries = (
        jnp.einsum("kglm,mkd->lkgd", grad_scores, rotated_keys, preferred_element_type=jnp.float32)
        * SCALE
    )
    grad_keys = (
        jnp.einsum("kglm,lkgd->mkd", grad_scores, query_rows, preferred_element_type=jnp.float32)
        * SCALE
    )
    return (grad_queries, grad_keys, grad_values)


def padded(matrix):
    return jnp.concatenate([jnp.zeros((1, matrix.shape[1]), matrix.dtype), matrix], axis=0)


def contract_rows(left, right):
    return lax.dot_general(
        left, right, (((0,), (0,)), ((), ())), preferred_element_type=jnp.float32
    )


def unit_activity(rows_in, gate_w, up_w):
    gate_activation = jnp.einsum(
        "nrd,ndf->nrf", rows_in, gate_w, preferred_element_type=jnp.float32
    )
    up_activation = jnp.einsum("nrd,ndf->nrf", rows_in, up_w, preferred_element_type=jnp.float32)
    sigmoid_gate = jax.nn.sigmoid(gate_activation)
    swish = gate_activation * sigmoid_gate
    return (gate_activation, up_activation, sigmoid_gate, swish)


def unit_backward(grad_in, down_w, gate_activation, up_activation, sigmoid_gate, swish):
    grad_inner = jnp.einsum("nrd,nfd->nrf", grad_in, down_w, preferred_element_type=jnp.float32)
    gate_grad = (
        grad_inner * up_activation * sigmoid_gate * (1.0 + gate_activation * (1.0 - sigmoid_gate))
    ).astype(jnp.bfloat16)
    up_grad = (grad_inner * swish).astype(jnp.bfloat16)
    return (gate_grad, up_grad)


def local(
    tokens,
    norm1_gain,
    w_query,
    key_projection_weight,
    value_projection_weight,
    w_output,
    norm2_gain,
    w_router,
    expert_gate_weight,
    expert_up_weight,
    expert_down_weight,
    expert_ids,
    cotangent,
):
    tok_count = tokens.shape[0]
    model_width = tokens.shape[1]
    experts = w_router.shape[1]
    top_count = expert_ids.shape[1]
    heads_query = w_query.shape[1] // HEAD_DIMENSION
    heads_kv = key_projection_weight.shape[1] // HEAD_DIMENSION
    group_size = heads_query // heads_kv
    sequences = tok_count // SEQ_LEN
    cosine, sine_table = tables(tok_count)
    highest_prec = lax.Precision.HIGHEST
    tensor_count = lax.axis_size("tensor")
    tensor_index = lax.axis_index("tensor")
    col_width = model_width // tensor_count
    col_start = tensor_index * col_width
    share = CAP // tensor_count
    resid_in = tokens.astype(jnp.float32)
    first_scale = lax.rsqrt(jnp.mean(resid_in * resid_in, axis=-1, keepdims=True) + EPS)
    first_norm = (resid_in * first_scale * norm1_gain).astype(jnp.bfloat16)
    query_raw = jnp.dot(first_norm, w_query, preferred_element_type=jnp.float32).reshape(
        tok_count, heads_query, HEAD_DIMENSION
    )
    key_raw = jnp.dot(
        first_norm, key_projection_weight, preferred_element_type=jnp.float32
    ).reshape(tok_count, heads_kv, HEAD_DIMENSION)
    query_rows = (
        rotate(query_raw, cosine, sine_table, 1.0)
        .astype(jnp.bfloat16)
        .reshape(sequences, SEQ_LEN, heads_kv, group_size, HEAD_DIMENSION)
    )
    rotated_keys = (
        rotate(key_raw, cosine, sine_table, 1.0)
        .astype(jnp.bfloat16)
        .reshape(sequences, SEQ_LEN, heads_kv, HEAD_DIMENSION)
    )
    value_rows = (
        jnp.dot(first_norm, value_projection_weight, preferred_element_type=jnp.float32)
        .astype(jnp.bfloat16)
        .reshape(sequences, SEQ_LEN, heads_kv, HEAD_DIMENSION)
    )
    attended, log_total = lax.map(attend_forward, (query_rows, rotated_keys, value_rows))
    attended = attended.reshape(tok_count, heads_query * HEAD_DIMENSION)
    branch = lax.psum(jnp.dot(attended, w_output, preferred_element_type=jnp.float32), "tensor")
    hidden = resid_in + branch
    second_scale = lax.rsqrt(jnp.mean(hidden * hidden, axis=-1, keepdims=True) + EPS)
    second_norm = (hidden * second_scale * norm2_gain).astype(jnp.bfloat16)
    logits = jnp.dot(second_norm, w_router, preferred_element_type=jnp.float32)
    chosen = jnp.take_along_axis(logits, expert_ids, axis=1)
    routing = jax.nn.softmax(chosen, axis=-1)
    one_hot = (
        expert_ids[:, :, None] == jnp.arange(experts, dtype=jnp.int32)[None, None, :]
    ).astype(jnp.int32)
    flat_hot = one_hot.reshape(tok_count * top_count, experts)
    slot_index = jnp.sum((jnp.cumsum(flat_hot, axis=0) - flat_hot) * flat_hot, axis=-1)
    slot_place = expert_ids.reshape(-1) * CAP + slot_index
    slot_owner = (
        jnp.zeros((experts * CAP,), jnp.int32)
        .at[slot_place]
        .set(jnp.arange(tok_count * top_count, dtype=jnp.int32) + 1)
    )
    owner_grid = slot_owner.reshape(experts, share, tensor_count)
    owner_mine = lax.dynamic_index_in_dim(owner_grid, tensor_index, 2, keepdims=False).reshape(-1)
    token_mine = jnp.where(owner_mine > 0, (owner_mine - 1) // top_count + 1, 0)
    gate_mine = jnp.concatenate([jnp.zeros((1,), jnp.float32), routing.reshape(-1)])[owner_mine]
    grad_out = cotangent.astype(jnp.float32)
    hidden_cols = lax.dynamic_slice_in_dim(hidden, col_start, col_width, 1)
    outgoing = padded(second_norm)[token_mine].reshape(experts, share, model_width)
    input_rows = lax.all_to_all(outgoing, "expert", split_axis=0, concat_axis=1, tiled=True)
    gate_full, up_full = (
        lax.all_gather(expert_gate_weight, "tensor", axis=2, tiled=True),
        lax.all_gather(expert_up_weight, "tensor", axis=2, tiled=True),
    )
    down_full = lax.all_gather(expert_down_weight, "tensor", axis=1, tiled=True)
    gate_activation, up_activation, sigmoid_gate, swish = unit_activity(
        input_rows, gate_full, up_full
    )
    inner_activation = (swish * up_activation).astype(jnp.bfloat16)
    expert_out = jnp.einsum(
        "nrf,nfd->nrd", inner_activation, down_full, preferred_element_type=jnp.float32
    ).astype(jnp.bfloat16)
    returned = (
        lax.all_to_all(expert_out, "expert", split_axis=1, concat_axis=0, tiled=True)
        .reshape(experts * share, model_width)
        .astype(jnp.float32)
    )
    weighted = returned * gate_mine[:, None]
    routed_part = (
        jnp.zeros((tok_count + 1, model_width), jnp.float32).at[token_mine].add(weighted)[1:]
    )
    routed_cols = lax.psum_scatter(
        routed_part.astype(jnp.bfloat16), "tensor", scatter_dimension=1, tiled=True
    ).astype(jnp.float32)
    mixed = (hidden_cols + routed_cols).astype(jnp.bfloat16)
    grad_picked = padded(grad_out)[token_mine]
    routing_slot = jnp.sum(grad_picked * returned, axis=-1)
    routing_part = (
        jnp.zeros((tok_count * top_count + 1,), jnp.float32)
        .at[owner_mine]
        .add(routing_slot)[1:]
        .reshape(tok_count, top_count)
    )
    grad_send = (
        (grad_picked * gate_mine[:, None]).astype(jnp.bfloat16).reshape(experts, share, model_width)
    )
    grad_in_rows = lax.all_to_all(grad_send, "expert", split_axis=0, concat_axis=1, tiled=True)
    gate_grad, up_grad = unit_backward(
        grad_in_rows, down_full, gate_activation, up_activation, sigmoid_gate, swish
    )
    gate_total = jnp.einsum(
        "nrd,nrf->ndf", input_rows, gate_grad, preferred_element_type=jnp.float32
    )
    up_total = jnp.einsum("nrd,nrf->ndf", input_rows, up_grad, preferred_element_type=jnp.float32)
    down_total = jnp.einsum(
        "nrf,nrd->nfd", inner_activation, grad_in_rows, preferred_element_type=jnp.float32
    )
    grad_gate, up_weight_gradient = (
        lax.psum_scatter(
            gate_total.astype(jnp.bfloat16), "tensor", scatter_dimension=2, tiled=True
        ).astype(jnp.float32),
        lax.psum_scatter(
            up_total.astype(jnp.bfloat16), "tensor", scatter_dimension=2, tiled=True
        ).astype(jnp.float32),
    )
    grad_down = lax.psum_scatter(
        down_total.astype(jnp.bfloat16), "tensor", scatter_dimension=1, tiled=True
    ).astype(jnp.float32)
    grad_rows_out = jnp.einsum(
        "nrf,ndf->nrd", gate_grad, gate_full, preferred_element_type=jnp.float32
    )
    grad_rows_out = (
        grad_rows_out
        + jnp.einsum("nrf,ndf->nrd", up_grad, up_full, preferred_element_type=jnp.float32)
    ).astype(jnp.bfloat16)
    grad_returned = (
        lax.all_to_all(grad_rows_out, "expert", split_axis=1, concat_axis=0, tiled=True)
        .reshape(experts * share, model_width)
        .astype(jnp.float32)
    )
    grad_norm_part = (
        jnp.zeros((tok_count + 1, model_width), jnp.float32).at[token_mine].add(grad_returned)[1:]
    )
    grad_norm_rows, grad_routing = lax.psum((grad_norm_part, routing_part), "tensor")
    grad_chosen = routing * (grad_routing - jnp.sum(routing * grad_routing, axis=-1, keepdims=True))
    grad_logits = jnp.einsum(
        "sk,ske->se", grad_chosen, one_hot.astype(jnp.float32), precision=highest_prec
    )
    router_float = w_router.astype(jnp.float32)
    grad_second = grad_norm_rows + jnp.dot(grad_logits, router_float.T, precision=highest_prec)
    grad_router = jnp.dot(second_norm.astype(jnp.float32).T, grad_logits, precision=highest_prec)
    gained_two = grad_second * norm2_gain
    grad_norm2 = jnp.sum(grad_second * hidden * second_scale, axis=0)
    grad_hidden = (
        grad_out
        + second_scale * gained_two
        - hidden * second_scale**3 * jnp.mean(gained_two * hidden, axis=-1, keepdims=True)
    )
    grad_branch = grad_hidden.astype(jnp.bfloat16)
    grad_output = contract_rows(attended, grad_branch)
    grad_heads = jnp.dot(grad_branch, w_output.T, preferred_element_type=jnp.float32).astype(
        jnp.bfloat16
    )
    grad_heads = grad_heads.reshape(sequences, SEQ_LEN, heads_kv, group_size, HEAD_DIMENSION)
    grad_queries, grad_keys, grad_values = lax.map(
        attend_backward, (query_rows, rotated_keys, value_rows, grad_heads, log_total)
    )
    grad_query_raw = rotate(
        grad_queries.reshape(tok_count, heads_query, HEAD_DIMENSION), cosine, sine_table, -1.0
    )
    grad_query_raw = grad_query_raw.reshape(tok_count, heads_query * HEAD_DIMENSION).astype(
        jnp.bfloat16
    )
    grad_key_raw = rotate(
        grad_keys.reshape(tok_count, heads_kv, HEAD_DIMENSION), cosine, sine_table, -1.0
    )
    grad_key_raw = grad_key_raw.reshape(tok_count, heads_kv * HEAD_DIMENSION).astype(jnp.bfloat16)
    grad_value_raw = grad_values.reshape(tok_count, heads_kv * HEAD_DIMENSION).astype(jnp.bfloat16)
    grad_query = contract_rows(first_norm, grad_query_raw)
    grad_key = contract_rows(first_norm, grad_key_raw)
    grad_value = contract_rows(first_norm, grad_value_raw)
    grad_first_part = jnp.dot(grad_query_raw, w_query.T, preferred_element_type=jnp.float32)
    grad_first_part = grad_first_part + jnp.dot(
        grad_key_raw, key_projection_weight.T, preferred_element_type=jnp.float32
    )
    grad_first_part = grad_first_part + jnp.dot(
        grad_value_raw, value_projection_weight.T, preferred_element_type=jnp.float32
    )
    grad_first = lax.psum(grad_first_part.astype(jnp.bfloat16), "tensor").astype(jnp.float32)
    gained_one = grad_first * norm1_gain
    grad_norm1 = jnp.sum(grad_first * resid_in * first_scale, axis=0)
    grad_input = (
        grad_hidden
        + first_scale * gained_one
        - resid_in * first_scale**3 * jnp.mean(gained_one * resid_in, axis=-1, keepdims=True)
    )
    summed = (
        lax.psum(grad_query.astype(jnp.bfloat16), "expert").astype(jnp.float32),
        lax.psum(grad_key.astype(jnp.bfloat16), "expert").astype(jnp.float32),
        lax.psum(grad_value.astype(jnp.bfloat16), "expert").astype(jnp.float32),
        lax.psum(grad_output.astype(jnp.bfloat16), "expert").astype(jnp.float32),
        lax.psum(grad_router.astype(jnp.bfloat16), "expert").astype(jnp.float32),
        lax.psum(grad_norm1.astype(jnp.bfloat16), "expert").astype(jnp.float32),
        lax.psum(grad_norm2.astype(jnp.bfloat16), "expert").astype(jnp.float32),
    )
    return (
        mixed,
        grad_input,
        summed[5],
        summed[0],
        summed[1],
        summed[2],
        summed[3],
        summed[6],
        summed[4],
        grad_gate,
        up_weight_gradient,
        grad_down,
    )


def solution(mesh):
    placed = (
        P("expert", None),
        P(),
        P(None, "tensor"),
        P(None, "tensor"),
        P(None, "tensor"),
        P("tensor", None),
        P(),
        P(),
        P("expert", None, "tensor"),
        P("expert", None, "tensor"),
        P("expert", "tensor", None),
        P("expert", None),
        P("expert", None),
    )
    return jax.shard_map(
        local,
        mesh=mesh,
        in_specs=placed,
        out_specs=(
            P("expert", "tensor"),
            P("expert", None),
            P(),
            P(None, "tensor"),
            P(None, "tensor"),
            P(None, "tensor"),
            P("tensor", None),
            P(),
            P(),
            P("expert", None, "tensor"),
            P("expert", None, "tensor"),
            P("expert", "tensor", None),
        ),
        check_vma=False,
    )
```

profile of v0, /device:TPU:0, one launch (start us, length us, event | category | flops | bytes accessed | tf_op | source)
XLA Modules:
  0.0 1028.5 jit_solution(11154208974896947743)
XLA Ops:
  22.8 9.2 reduce-window.6
  34.2 15.5 %scatter_custom_fusion = s32[5120]{0:T(1024)S(1)} fusion(s32[4096]{0:T(1024)S(1)} %bitcast.225, s32[4096]{0:T(1024)S(1)} %iota_add_fusion, s32[]{:T(128)} %constant.87.clone.1), kind=kCustom, calls=%fused_computation.134 | custom fusion | bytes 20484 | tf_op jit(solution)/shard_map/scatter | solution.py:190
  51.4 58.3 %all-reduce.9.cloned.1.call-done = f32[512,1024]{1,0:T(8,128)} async-done(((f32[512,1024]{1,0:T(8,128)}), f32[512,1024]{1,0:T(8,128)}) %all-reduce.9.cloned.1.call-update) | async-done | bytes 2097168 | tf_op jit(solution)/shard_map/psum | solution.py:174
  119.6 36.4 %all_to_all.54 = bf16[32,40,1024]{2,1,0:T(8,128)(2,1)S(1)} all-to-all(bf16[32,40,1024]{2,1,0:T(8,128)(2,1)} %bitcast.199), channel_id=1, replica_groups=mesh['expert'=8,'tensor'=4] {'expert'}, dimensions={0} | all-to-all | bytes 5242880 | tf_op jit(solution)/shard_map/all_to_all | solution.py:199
  156.2 34.6 %all-gather.4.cloned.1.call-done = bf16[4,1024,512]{2,1,0:T(8,128)(2,1)} async-done(((bf16[4,1024,128]{2,1,0:T(8,128)(2,1)}), bf16[4,1024,512]{2,1,0:T(8,128)(2,1)}) %all-gather.4.cloned.1.call-update) | async-done | bytes 4194320 | tf_op jit(solution)/shard_map/all_gather | solution.py:201
  196.0 75.3 %all-gather.6.cloned.1.call-done = bf16[4,1024,512]{2,1,0:T(8,128)(2,1)} async-done(((bf16[4,1024,128]{2,1,0:T(8,128)(2,1)}), bf16[4,1024,512]{2,1,0:T(8,128)(2,1)}) %all-gather.6.cloned.1.call-update) | async-done | bytes 4194320 | tf_op jit(solution)/shard_map/all_gather | solution.py:202
  277.9 73.9 %all-gather.8.cloned.1.call-done = bf16[4,512,1024]{2,1,0:T(8,128)(2,1)} async-done(((bf16[4,128,1024]{2,1,0:T(8,128)(2,1)}), bf16[4,512,1024]{2,1,0:T(8,128)(2,1)}) %all-gather.8.cloned.1.call-update) | async-done | bytes 4194320 | tf_op jit(solution)/shard_map/all_gather | solution.py:204
  372.7 33.0 %gather_fusion.3 = f32[4096]{0:T(1024)S(1)} fusion(f32[512,32]{0,1:T(8,128)S(1)} %fusion.75, s32[4096]{0:T(1024)S(1)} %reshape.428), kind=kCustom, calls=%fused_computation.3 | custom fusion | bytes 65536 | tf_op jit(solution)/shard_map/jit(take_along_axis)/gather | solution.py:179
  412.7 8.9 scatter_custom_fusion.3
  421.9 16.0 %psum.79 = f32[512,8]{0,1:T(8,128)S(1)} all-reduce(f32[512,8]{0,1:T(8,128)S(1)} %copy.99), channel_id=1, replica_groups=mesh['expert'=8,'tensor'=4] {'tensor'}, use_global_device_ids=true, to_apply=%region_17.18 | all-reduce | flops 4096 | bytes 32768 | tf_op jit(solution)/shard_map/psum | solution.py:273
  438.3 7.1 gather_fusion.1
  448.3 36.6 %all_to_all.55 = bf16[32,40,1024]{2,1,0:T(8,128)(2,1)S(1)} all-to-all(bf16[32,40,1024]{2,1,0:T(8,128)(2,1)S(1)} %multiply_convert_fusion), channel_id=1, replica_groups=mesh['expert'=8,'tensor'=4] {'expert'}, dimensions={0} | all-to-all | bytes 5242880 | tf_op jit(solution)/shard_map/all_to_all | solution.py:236
  496.9 34.9 %all_to_all.56 = bf16[4,320,1024]{2,0,1:T(4,128)(2,1)S(1)} all-to-all(bf16[4,320,1024]{2,0,1:T(4,128)(2,1)S(1)} %copy.97), channel_id=1, replica_groups=mesh['expert'=8,'tensor'=4] {'expert'}, dimensions={1} | all-to-all | bytes 5242880 | tf_op jit(solution)/shard_map/all_to_all | solution.py:266
  535.2 15.2 %scatter_custom_fusion.2 = f32[513,1024]{1,0:T(8,128)S(1)} fusion(s32[1280]{0:T(1024)S(1)} %get-tuple-element.62, f32[1280,1024]{1,0:T(8,128)} %bitcast.200, f32[]{:T(128)} %constant.83.clone.1), kind=kCustom, calls=%fused_computation.78 | custom fusion | flops 1310720 | bytes 2101760 | tf_op jit(solution)/shard_map/scatter-add | solution.py:271
  558.2 16.1 %scatter_custom_fusion.1 = f32[513,1024]{1,0:T(8,128)} fusion(s32[1280]{0:T(1024)S(1)} %get-tuple-element.62, f32[1280,1024]{1,0:T(8,128)} %bitcast_multiply_fusion, f32[]{:T(128)} %constant.83.clone.1), kind=kCustom, calls=%fused_computation.80 | custom fusion | flops 1310720 | bytes 2101760 | tf_op jit(solution)/shard_map/scatter-add | solution.py:219
  580.1 54.7 %all-reduce.11.cloned.1.call-done = f32[512,1024]{1,0:T(8,128)} async-done(((f32[512,1024]{1,0:T(8,128)}), f32[512,1024]{1,0:T(8,128)}) %all-reduce.11.cloned.1.call-update) | async-done | bytes 2097168 | tf_op jit(solution)/shard_map/psum | solution.py:273
  661.8 8.1 copy.117
  682.1 8.1 copy.119
  706.0 21.7 %all-reduce.15.cloned.1.call-done = (bf16[1024,256]{1,0:T(8,128)(2,1)}, bf16[1024,128]{1,0:T(8,128)(2,1)}, bf16[1024,128]{1,0:T(8,128)(2,1)}, bf16[256,1024]{1,0:T(8,128)(2,1)}, bf16[1024,32]{0,1:T(8,128)(2,1)}) async-done(((bf16[1024,256]{1,0:T(8,128)(2,1)}, bf16[1024,128]{1,0:T(8,128)(2,1)}, bf16[1024,128]{1,0:T(8,128)(2,1)}, bf16[256,1024]{1,0:T(8,128)(2,1)}, bf16[1024,32]{0,1:T(8,128)(2,1)}), ...) | async-done | bytes 1638416 | tf_op jit(solution)/shard_map/psum | solution.py:327
  734.5 46.5 %all-reduce.13.cloned.1.call-done = bf16[512,1024]{1,0:T(8,128)(2,1)} async-done(((bf16[512,1024]{1,0:T(8,128)(2,1)}), bf16[512,1024]{1,0:T(8,128)(2,1)}) %all-reduce.13.cloned.1.call-update) | async-done | bytes 1048592 | tf_op jit(solution)/shard_map/psum | solution.py:318
  783.4 14.2 %all-reduce.2 = (bf16[1024]{0:T(1024)(128)(2,1)S(1)}, bf16[1024]{0:T(1024)(128)(2,1)S(1)}) all-reduce(bf16[1024]{0:T(1024)(128)(2,1)S(1)} %get-tuple-element.50, bf16[1024]{0:T(1024)(128)(2,1)S(1)} %get-tuple-element.48), channel_id=1, replica_groups=mesh['expert'=8,'tensor'=4] {'expert'}, use_global_device_ids=true, to_apply=%region_24.25 | all-reduce | flops 2048 | bytes 8192 | tf_op jit(solution)/shard_map/psum | solution.py:332
  802.3 57.3 %reduce-scatter.13.cloned.1.call-done = bf16[128,4096]{1,0:T(8,128)(2,1)} async-done(((bf16[512,4096]{1,0:T(8,128)(2,1)}), bf16[128,4096]{1,0:T(8,128)(2,1)}) %reduce-scatter.13.cloned.1.call-update) | async-done | bytes 1048592
  863.9 75.1 %reduce-scatter.15.cloned.1.call-done = bf16[128,4096]{1,0:T(8,128)(2,1)} async-done(((bf16[512,4096]{1,0:T(8,128)(2,1)}), bf16[128,4096]{1,0:T(8,128)(2,1)}) %reduce-scatter.15.cloned.1.call-update) | async-done | bytes 1048592
  943.4 75.4 %reduce-scatter.11.cloned.1.call-done = bf16[4,128,1024]{2,1,0:T(8,128)(2,1)} async-done(((bf16[4,512,1024]{2,1,0:T(8,128)(2,1)}), bf16[4,128,1024]{2,1,0:T(8,128)(2,1)}) %reduce-scatter.11.cloned.1.call-update) | async-done | bytes 1048592 | tf_op jit(solution)/shard_map/reduce_scatter | solution.py:255
  (276 shorter events, 180.8 us)
Async XLA Ops:
  7.2 11.4 %copy-start = (bf16[256,1024]{1,0:T(8,128)(2,1)S(1)}, bf16[256,1024]{1,0:T(8,128)(2,1)}, u32[]{:S(2)}) copy-start(bf16[256,1024]{1,0:T(8,128)(2,1)} %param.18) | copy-start | bytes 1572868
  7.2 102.4 %all-reduce.9.cloned.1.call-start = ((), (), s32[]{:S(2)}) async-start(), calls=%async_computation.8 | async-start | bytes 4194304 | tf_op jit(solution)/shard_map/psum | solution.py:174
  20.4 170.4 %all-gather.4.cloned.1.call-start = ((), (), s32[]{:S(2)}) async-start(), calls=%async_computation.9 | async-start | bytes 5242880 | tf_op jit(solution)/shard_map/all_gather | solution.py:201
  21.2 250.1 %all-gather.6.cloned.1.call-start = ((), (), s32[]{:S(2)}) async-start(), calls=%async_computation.10 | async-start | bytes 5242880 | tf_op jit(solution)/shard_map/all_gather | solution.py:202
  21.9 329.9 %all-gather.8.cloned.1.call-start = ((), (), s32[]{:S(2)}) async-start(), calls=%async_computation.11 | async-start | bytes 5242880 | tf_op jit(solution)/shard_map/all_gather | solution.py:204
  51.4 61.6 %copy-start.49 = (f32[1024]{0:T(1024)S(1)}, f32[1024]{0:T(1024)}, u32[]{:S(2)}) copy-start(f32[1024]{0:T(1024)} %param.19) | copy-start | bytes 12292
  156.2 115.1 %copy-start.2 = (bf16[4,8,40,1024]{3,2,1,0:T(8,128)(2,1)}, bf16[4,8,40,1024]{3,2,1,0:T(8,128)(2,1)S(1)}, u32[]{:S(2)}) copy-start(bf16[4,8,40,1024]{3,2,1,0:T(8,128)(2,1)S(1)} %copy.90) | copy-start | bytes 7864324
  359.4 46.7 %all-to-all-start.1 = ((bf16[4,320,1024]{2,0,1:T(4,128)(2,1)}), bf16[4,320,1024]{2,0,1:T(4,128)(2,1)}, u32[]{:S(2)}, u32[]{:S(2)}) async-start(bf16[4,320,1024]{2,0,1:T(4,128)(2,1)} %copy.91), calls=%async_computation.1 | async-start | bytes 5242880 | tf_op jit(solution)/shard_map/all_to_all | solution.py:213
  363.8 271.0 %all-reduce.11.cloned.1.call-start = ((), (), s32[]{:S(2)}) async-start(), calls=%async_computation.13 | async-start | bytes 4194304 | tf_op jit(solution)/shard_map/psum | solution.py:273
  448.3 36.9 %copy-start.23 = (f32[4,320,512]{2,1,0:T(8,128)S(1)}, f32[4,320,512]{2,1,0:T(8,128)}, u32[]{:S(2)}) copy-start(f32[4,320,512]{2,1,0:T(8,128)} %fusion.74) | copy-start | bytes 7864324
  448.3 36.9 %copy-start.63 = (f32[4,320,512]{2,1,0:T(8,128)S(1)}, f32[4,320,512]{2,1,0:T(8,128)}, u32[]{:S(2)}) copy-start(f32[4,320,512]{2,1,0:T(8,128)} %get-tuple-element.94) | copy-start | bytes 7864324
  551.9 152.2 %reduce-scatter.9.cloned.1.call-start = ((), (), s32[]{:S(2)}) async-start(), calls=%async_computation.12 | async-start | bytes 1310720 | tf_op jit(solution)/shard_map/reduce_scatter | solution.py:221
  574.3 60.6 %copy-start.5 = (f32[512,1024]{1,0:T(8,128)S(1)}, f32[512,1024]{1,0:T(8,128)}, u32[]{:S(2)}) copy-start(f32[512,1024]{1,0:T(8,128)} %copy-done.4) | copy-start | bytes 6291460
  574.3 60.6 %copy-start.50 = (f32[1024]{0:T(1024)S(1)}, f32[1024]{0:T(1024)}, u32[]{:S(2)}) copy-start(f32[1024]{0:T(1024)} %param.19) | copy-start | bytes 12292
  574.3 60.6 %copy-start.56 = (f32[512]{0:T(512)S(1)}, f32[512]{0:T(512)}, u32[]{:S(2)}) copy-start(f32[512]{0:T(512)} %copy-done.55) | copy-start | bytes 6148
  579.9 58.2 %copy-start.62 = (f32[512]{0:T(512)S(1)}, f32[512]{0:T(512)}, u32[]{:S(2)}) copy-start(f32[512]{0:T(512)} %get-tuple-element.89) | copy-start | bytes 6148
  579.9 147.8 %all-reduce.15.cloned.1.call-start = ((), (), s32[]{:S(2)}) async-start(), calls=%async_computation.18 | async-start | bytes 3276800 | tf_op jit(solution)/shard_map/psum | solution.py:327
  638.7 12.6 %copy-start.8 = (f32[512,1024]{1,0:T(8,128)}, f32[512,1024]{1,0:T(8,128)S(1)}, u32[]{:S(2)}) copy-start(f32[512,1024]{1,0:T(8,128)S(1)} %multiply_subtract_fusion) | copy-start | bytes 6291460
  652.7 128.4 %all-reduce.13.cloned.1.call-start = ((), (), s32[]{:S(2)}) async-start(), calls=%async_computation.14 | async-start | bytes 2097152 | tf_op jit(solution)/shard_map/psum | solution.py:318
  655.6 204.1 %reduce-scatter.13.cloned.1.call-start = ((), (), s32[]{:S(2)}) async-start(), calls=%async_computation.16 | async-start | bytes 5242880
  676.3 262.7 %reduce-scatter.15.cloned.1.call-start = ((), (), s32[]{:S(2)}) async-start(), calls=%async_computation.17 | async-start | bytes 5242880
  696.7 322.1 %reduce-scatter.11.cloned.1.call-start = ((), (), s32[]{:S(2)}) async-start(), calls=%async_computation.15 | async-start | bytes 5242880 | tf_op jit(solution)/shard_map/reduce_scatter | solution.py:255
  729.9 69.0 %copy-start.9 = (f32[512,1024]{1,0:T(8,128)S(1)}, f32[512,1024]{1,0:T(8,128)}, u32[]{:S(2)}) copy-start(f32[512,1024]{1,0:T(8,128)} %copy-done.8) | copy-start | bytes 6291460
  729.9 69.0 %copy-start.61 = (f32[512]{0:T(512)S(1)}, f32[512]{0:T(512)}, u32[]{:S(2)}) copy-start(f32[512]{0:T(512)} %get-tuple-element.87) | copy-start | bytes 6148
  (52 other events, 130.0 us)
Sparse Core Ops, SparseCore 0:
  20.5 89.0 all-reduce.8
  111.3 79.5 all-gather.3
  192.5 78.7 all-gather.5
  272.8 78.9 all-gather.7
  552.0 82.7 all-reduce.10
  637.6 26.0 reduce-scatter.8
  668.6 59.0 all-reduce.14
  730.1 50.9 all-reduce.12
  783.4 76.1 reduce-scatter.12
  861.8 77.2 reduce-scatter.14
  941.5 77.2 reduce-scatter.10
where the time goes:
time: 1040 us; the launch traced here: 1030 us
  waiting for transfers between devices  575 us (55%)
  blocking collectives  138 us (13%)
  local copies, waits for them, and re-layouts  136 us (13%)
  other arithmetic  93.1 us (9%)
  matrix products  64.9 us (6%)
  between operations  15.5 us (1%)
    unnamed x13, waiting for transfers between devices  134 us
    reduce_scatter x1, waiting for transfers between devices, local(): lax.psum_scatter(down_total.astype(jnp.bfloat16), 'tensor', scatter_dimen...  75.4 us
    all_gather x1, waiting for transfers between devices, local(): lax.all_gather(expert_up_weight, 'tensor', axis=2, tiled=True)  75.3 us
    all_gather x1, waiting for transfers between devices, local(): down_full = lax.all_gather(expert_down_weight, 'tensor', axis=1, tiled=True)  73.9 us
    psum x1, waiting for transfers between devices, local(): lax.psum(jnp.dot(attended, w_output, preferred_element_type=jnp.float32),...  58.3 us
    psum x1, waiting for transfers between devices, local(): lax.psum((grad_norm_part, routing_part), 'tensor')  54.7 us
    unnamed x137, local copies, waits for them, and re-layouts  46.9 us
    psum x1, waiting for transfers between devices, local(): lax.psum(grad_first_part.astype(jnp.bfloat16), 'tensor').astype(jnp.float32)  46.5 us
  transfers between devices with their start and end apart: 12, of which 10 were waited for; matrix products, arithmetic and copies ran while one was open for 20% of the time, Pallas kernels for 0%

commit v1 on v0

v1 whole, which is shorter than its diff:
```python
import math

import jax
import jax.numpy as jnp
from jax import lax
from jax.sharding import PartitionSpec as P

HEAD_DIMENSION = 64
SEQ_LEN = 512

EPS = 1e-06
SCALE = 0.125
NEGATIVE = -1e30
THETA = 10000.0
F32 = jnp.float32
BF16 = jnp.bfloat16
EXACT = lax.Precision.HIGHEST


def tables(tok_count):
    half = HEAD_DIMENSION // 2
    freq = jnp.exp(-math.log(THETA) * jnp.arange(half, dtype=F32) / half)
    places = (jnp.arange(tok_count) % SEQ_LEN).astype(F32)
    angle = places[:, None] * freq[None, :]
    return (jnp.cos(angle)[:, None, :], jnp.sin(angle)[:, None, :])


def rotate(field, cosine, sine_table, factor):
    half = HEAD_DIMENSION // 2
    first = field[..., :half]
    second = field[..., half:]
    return jnp.concatenate(
        [
            first * cosine - factor * second * sine_table,
            second * cosine + factor * first * sine_table,
        ],
        axis=-1,
    )


def causal_mask():
    places = jnp.arange(SEQ_LEN)
    return places[:, None] >= places[None, :]


def attend_forward(query_rows, rotated_keys, value_rows):
    scores = (
        jnp.einsum("lkgd,mkd->kglm", query_rows, rotated_keys, preferred_element_type=F32) * SCALE
    )
    scores = jnp.where(causal_mask(), scores, NEGATIVE)
    highest = jnp.max(scores, axis=-1, keepdims=True)
    expanded = jnp.exp(scores - highest)
    summed = jnp.sum(expanded, axis=-1, keepdims=True)
    probability = (expanded / summed).astype(BF16)
    heads_out = jnp.einsum("kglm,mkd->lkgd", probability, value_rows, preferred_element_type=F32)
    return (heads_out.astype(BF16), (highest + jnp.log(summed))[..., 0])


def attend_backward(query_rows, rotated_keys, value_rows, grad_heads, log_total):
    scores = (
        jnp.einsum("lkgd,mkd->kglm", query_rows, rotated_keys, preferred_element_type=F32) * SCALE
    )
    probability = jnp.where(causal_mask(), jnp.exp(scores - log_total[..., None]), 0.0)
    prob_low = probability.astype(BF16)
    grad_values = jnp.einsum("kglm,lkgd->mkd", prob_low, grad_heads, preferred_element_type=F32)
    grad_prob = jnp.einsum("lkgd,mkd->kglm", grad_heads, value_rows, preferred_element_type=F32)
    row_delta = jnp.sum(probability * grad_prob, axis=-1, keepdims=True)
    grad_scores = (probability * (grad_prob - row_delta)).astype(BF16)
    grad_queries = (
        jnp.einsum("kglm,mkd->lkgd", grad_scores, rotated_keys, preferred_element_type=F32) * SCALE
    )
    grad_keys = (
        jnp.einsum("kglm,lkgd->mkd", grad_scores, query_rows, preferred_element_type=F32) * SCALE
    )
    return (grad_queries, grad_keys, grad_values)


def mm(left, right):
    return jnp.dot(left, right, preferred_element_type=F32)


def mm_rows(left, right):
    return lax.dot_general(left, right, (((0,), (0,)), ((), ())), preferred_element_type=F32)


def mm_cols(left, right):
    return lax.dot_general(left, right, (((1,), (1,)), ((), ())), preferred_element_type=F32)


def piece(array, index, size, axis=0):
    return lax.dynamic_slice_in_dim(array, index * size, size, axis)


def swap(array, mask):
    size = lax.axis_size("expert")
    return lax.ppermute(array, "expert", [(i, i ^ mask) for i in range(size)])


def z_shift(array, step):
    size = lax.axis_size("tensor")
    return lax.ppermute(array, "tensor", [(i, (i + step) % size) for i in range(size)])


def z_received(array):
    return [array] + [z_shift(array, step) for step in range(1, lax.axis_size("tensor"))]


def z_gather(array):
    size, mine = lax.axis_size("tensor"), lax.axis_index("tensor")
    rows = array.shape[0]
    whole = jnp.zeros((rows * size,) + array.shape[1:], array.dtype)
    for step, part in enumerate(z_received(array)):
        whole = lax.dynamic_update_slice_in_dim(whole, part, (mine + size - step) % size * rows, 0)
    return whole


def z_scatter(array, axis=0):
    size, mine = lax.axis_size("tensor"), lax.axis_index("tensor")
    width = array.shape[axis] // size
    total = piece(array, mine, width, axis).astype(F32)
    for step in range(1, size):
        sent = piece(array, (mine + step) % size, width, axis).astype(BF16)
        total = total + z_shift(sent, step).astype(F32)
    return total


def same_core_groups():
    size = lax.axis_size("expert")
    return [list(range(0, size, 2)), list(range(1, size, 2))]


def plane_gather(array):
    if lax.axis_size("expert") != 8:
        return [
            lax.all_gather(
                array, "expert", axis=0, tiled=True, axis_index_groups=same_core_groups()
            )
        ]
    half = array.shape[0] // 2
    from_x = swap(array, 2)
    from_y = swap(array, 4)
    diagonal = jnp.concatenate([swap(from_x[:half], 4), swap(from_y[half:], 2)])
    return [array, from_x, from_y, diagonal]


def plane_scatter(blocks):
    if lax.axis_size("expert") != 8:
        return lax.psum_scatter(
            blocks[0].astype(BF16),
            "expert",
            scatter_dimension=0,
            tiled=True,
            axis_index_groups=same_core_groups(),
        ).astype(F32)
    own, for_x, for_y, diagonal = blocks
    half = own.shape[0] // 2
    diagonal = diagonal.astype(BF16)
    via_x = swap(diagonal[:half], 2).astype(F32)
    via_y = swap(diagonal[half:], 4).astype(F32)
    for_y = jnp.concatenate([for_y[:half] + via_x, for_y[half:]]).astype(BF16)
    for_x = jnp.concatenate([for_x[:half], for_x[half:] + via_y]).astype(BF16)
    return own + swap(for_x, 2).astype(F32) + swap(for_y, 4).astype(F32)


def expert_sum(array):
    if lax.axis_size("expert") != 8:
        return lax.psum(array.astype(BF16), "expert").astype(F32)
    place = lax.axis_index("expert")
    core, chip = place % 2, place // 2
    half = array.shape[0] // 2
    rows = half // 4
    mine = piece(array, core, half) + swap(
        piece(array, 1 - core, half).astype(BF16), 1
    ).astype(F32)
    total = piece(mine, chip, rows)
    for mask in (1, 2, 3):
        total = total + swap(piece(mine, chip ^ mask, rows).astype(BF16), 2 * mask).astype(F32)
    total = total.astype(BF16)
    gathered = jnp.zeros((half,) + array.shape[1:], BF16)
    for mask in (0, 1, 2, 3):
        part = swap(total, 2 * mask) if mask else total
        gathered = lax.dynamic_update_slice_in_dim(gathered, part, (chip ^ mask) * rows, 0)
    both = jnp.concatenate([gathered, gathered])
    both = lax.dynamic_update_slice_in_dim(both, swap(gathered, 1), (1 - core) * half, 0)
    return both.astype(F32)


def small_sum(array, over_tensor):
    size = lax.axis_size("expert")
    if size & (size - 1):
        array = lax.psum(array, "expert")
    else:
        mask = 1
        while mask < size:
            array = array + swap(array, mask)
            mask *= 2
    if over_tensor:
        parts = z_received(array)
        array = parts[0]
        for part in parts[1:]:
            array = array + part
    return array


def norm_scale(field):
    return lax.rsqrt(jnp.mean(field * field, axis=-1, keepdims=True) + EPS)


def route(normed, router, chosen):
    logits = mm(normed, router)
    masked = jnp.where(chosen, logits, NEGATIVE)
    highest = jnp.max(masked, axis=-1, keepdims=True)
    expanded = jnp.where(chosen, jnp.exp(masked - highest), 0.0)
    return expanded / jnp.sum(expanded, axis=-1, keepdims=True)


def local(
    tokens,
    norm1_gain,
    w_query,
    key_projection_weight,
    value_projection_weight,
    w_output,
    norm2_gain,
    w_router,
    expert_gate_weight,
    expert_up_weight,
    expert_down_weight,
    expert_ids,
    cotangent,
):
    tok_count = tokens.shape[0]
    model_width = tokens.shape[1]
    experts = w_router.shape[1]
    here, units = expert_gate_weight.shape[0], expert_gate_weight.shape[2]
    heads_query = w_query.shape[1] // HEAD_DIMENSION
    heads_kv = key_projection_weight.shape[1] // HEAD_DIMENSION
    group_size = heads_query // heads_kv
    cosine, sine_table = tables(tok_count)
    expert_count = lax.axis_size("expert")
    tensor_count = lax.axis_size("tensor")
    expert_place = lax.axis_index("expert")
    tensor_place = lax.axis_index("tensor")
    core = expert_place % 2
    own_rows = tok_count // tensor_count
    col_width = model_width // tensor_count

    ids_blocks = plane_gather(expert_ids.T) if expert_count == 8 else [
        lax.all_gather(
            expert_ids, "expert", axis=0, tiled=True, axis_index_groups=same_core_groups()
        ).T
    ]
    grad_blocks = plane_gather(cotangent)

    def chip_weights(weight):
        other = swap(weight, 1)
        return jnp.concatenate([weight, other])

    def as_columns(weight):
        return weight.transpose(1, 0, 2).reshape(model_width, -1)

    gate_w = as_columns(chip_weights(expert_gate_weight))
    up_w = as_columns(chip_weights(expert_up_weight))
    down_w = chip_weights(expert_down_weight).reshape(-1, model_width)

    share = w_output.shape[0] // expert_count
    w_piece = piece(w_output, expert_place, share)
    w_pieces = jnp.stack([z_shift(w_piece, step) for step in range(1, tensor_count)])
    if expert_count == 8:
        w_other = swap(w_pieces, 1)
        w_pair = jnp.where(
            core == 0,
            jnp.concatenate([w_pieces, w_other], axis=1),
            jnp.concatenate([w_other, w_pieces], axis=1),
        )
        chip = expert_place // 2
        w_parts = jnp.zeros((tensor_count - 1,) + w_output.shape, BF16)
        w_x = swap(w_pair, 2)
        w_y = swap(w_pair, 4)
        w_d = jnp.concatenate([swap(w_x[:, :share], 4), swap(w_y[:, share:], 2)], axis=1)
        for mask, part in enumerate((w_pair, w_x, w_y, w_d)):
            w_parts = lax.dynamic_update_slice_in_dim(w_parts, part, (chip ^ mask) * 2 * share, 1)
    else:
        w_parts = lax.all_gather(w_pieces, "expert", axis=1, tiled=True)

    resid_in = tokens.astype(F32)
    first_scale = norm_scale(resid_in)
    first_norm = (resid_in * first_scale * norm1_gain).astype(BF16)
    query_raw = mm(first_norm, w_query).reshape(tok_count, heads_query, HEAD_DIMENSION)
    key_raw = mm(first_norm, key_projection_weight).reshape(tok_count, heads_kv, HEAD_DIMENSION)
    query_rows = (
        rotate(query_raw, cosine, sine_table, 1.0)
        .astype(BF16)
        .reshape(tok_count, heads_kv, group_size, HEAD_DIMENSION)
    )
    rotated_keys = rotate(key_raw, cosine, sine_table, 1.0).astype(BF16)
    value_rows = (
        mm(first_norm, value_projection_weight)
        .astype(BF16)
        .reshape(tok_count, heads_kv, HEAD_DIMENSION)
    )
    attended, log_total = attend_forward(query_rows, rotated_keys, value_rows)
    attended = attended.reshape(tok_count, heads_query * HEAD_DIMENSION)

    attended_parts = z_received(attended)
    hidden = resid_in + mm(attended, w_output)
    for step in range(1, tensor_count):
        hidden = hidden + mm(attended_parts[step], w_parts[step - 1])
    second_scale = norm_scale(hidden)
    second_norm = (hidden * second_scale * norm2_gain).astype(BF16)

    names = jnp.arange(experts, dtype=jnp.int32)
    first_here = expert_place * here
    first_other = (expert_place ^ 1) * here
    out_blocks, row_blocks, routing_blocks = [], [], []
    gate_total = up_total = down_total = 0.0
    for normed, grad, ids in zip(plane_gather(second_norm), grad_blocks, ids_blocks):
        rows = normed.shape[0]
        chosen = jnp.any(ids.T[:, :, None] == names[None, None, :], axis=1)
        routing = route(normed, w_router, chosen)
        weight = jnp.concatenate(
            [
                lax.dynamic_slice_in_dim(routing, first_here, here, 1),
                lax.dynamic_slice_in_dim(routing, first_other, here, 1),
            ],
            axis=1,
        )
        wide = jnp.repeat(weight, units, axis=1)
        gate_act = mm(normed, gate_w)
        up_act = mm(normed, up_w)
        grad_plain = mm_cols(grad, down_w)
        sigmoid_gate = jax.nn.sigmoid(gate_act)
        swish = gate_act * sigmoid_gate
        inner = swish * up_act
        grad_inner = grad_plain * wide
        routing_blocks.append(
            jnp.sum((inner * grad_plain).reshape(rows, 2 * here, units), axis=-1)
        )
        inner_low = (inner * wide).astype(BF16)
        gate_grad = (
            grad_inner * up_act * sigmoid_gate * (1.0 + gate_act * (1.0 - sigmoid_gate))
        ).astype(BF16)
        up_grad = (grad_inner * swish).astype(BF16)
        out_blocks.append(mm(inner_low, down_w))
        row_blocks.append(mm_cols(gate_grad, gate_w) + mm_cols(up_grad, up_w))
        gate_total = gate_total + mm_rows(normed, gate_grad)
        up_total = up_total + mm_rows(normed, up_grad)
        down_total = down_total + mm_rows(inner_low, grad)

    row_sum = z_scatter(plane_scatter(row_blocks))

    if expert_count == 8:
        grad_routing = jnp.zeros((experts, tok_count), F32)
        for mask, block in enumerate(routing_blocks):
            part = block.T
            part = swap(part, 2 * mask) if mask else part
            source = (expert_place ^ (2 * mask)) * here
            source_other = (expert_place ^ (2 * mask) ^ 1) * here
            grad_routing = lax.dynamic_update_slice_in_dim(grad_routing, part[:here], source, 0)
            grad_routing = lax.dynamic_update_slice_in_dim(
                grad_routing, part[here:], source_other, 0
            )
    else:
        block = routing_blocks[0]
        spread = jnp.zeros((block.shape[0], experts), F32)
        spread = lax.dynamic_update_slice_in_dim(spread, block[:, :here], first_here, 1)
        spread = lax.dynamic_update_slice_in_dim(spread, block[:, here:], first_other, 1)
        grad_routing = lax.psum_scatter(
            spread,
            "expert",
            scatter_dimension=0,
            tiled=True,
            axis_index_groups=same_core_groups(),
        ).T
    routing_parts = z_received(grad_routing)
    grad_routing = routing_parts[0]
    for part in routing_parts[1:]:
        grad_routing = grad_routing + part
    grad_routing = grad_routing.T
    own_chosen = jnp.any(expert_ids[:, :, None] == names[None, None, :], axis=1)
    own_routing = route(second_norm, w_router, own_chosen)
    grad_logits = own_routing * (
        grad_routing - jnp.sum(own_routing * grad_routing, axis=-1, keepdims=True)
    )

    def mine(array):
        return piece(array, tensor_place, own_rows)

    my_logits, my_hidden, my_scale = mine(grad_logits), mine(hidden), mine(second_scale)
    my_normed = mine(second_norm).astype(F32)
    router_float = w_router.astype(F32)
    grad_second = row_sum + jnp.dot(my_logits, router_float.T, precision=EXACT)
    grad_router = lax.dot_general(
        my_logits, my_normed, (((0,), (0,)), ((), ())), precision=EXACT
    )
    grad_norm2 = jnp.sum(grad_second * my_hidden * my_scale, axis=0)
    gained_two = grad_second * norm2_gain
    my_grad_hidden = (
        mine(cotangent).astype(F32)
        + my_scale * gained_two
        - my_hidden * my_scale**3 * jnp.mean(gained_two * my_hidden, axis=-1, keepdims=True)
    )
    grad_branch = z_gather(my_grad_hidden.astype(BF16))
    early = small_sum(jnp.concatenate([grad_router, grad_norm2[None]]), True)
    grad_output = expert_sum(mm_rows(attended, grad_branch))

    grad_heads = mm_cols(grad_branch, w_output).astype(BF16)
    grad_heads = grad_heads.reshape(tok_count, heads_kv, group_size, HEAD_DIMENSION)
    grad_queries, grad_keys, grad_values = attend_backward(
        query_rows, rotated_keys, value_rows, grad_heads, log_total
    )
    grad_query_raw = rotate(
        grad_queries.reshape(tok_count, heads_query, HEAD_DIMENSION), cosine, sine_table, -1.0
    )
    grad_query_raw = grad_query_raw.reshape(tok_count, -1).astype(BF16)
    grad_key_raw = rotate(grad_keys, cosine, sine_table, -1.0)
    grad_key_raw = grad_key_raw.reshape(tok_count, -1).astype(BF16)
    grad_value_raw = grad_values.reshape(tok_count, -1).astype(BF16)
    grad_raw = jnp.concatenate([grad_query_raw, grad_key_raw, grad_value_raw], axis=1)
    grad_weights = expert_sum(mm_rows(first_norm, grad_raw))
    q_width, k_width = w_query.shape[1], key_projection_weight.shape[1]
    grad_first = (
        mm_cols(grad_query_raw, w_query)
        + mm_cols(grad_key_raw, key_projection_weight)
        + mm_cols(grad_value_raw, value_projection_weight)
    )
    grad_first = z_scatter(grad_first)
    gained_one = grad_first * norm1_gain
    my_resid, my_first_scale = mine(resid_in), mine(first_scale)
    grad_norm1 = jnp.sum(grad_first * my_resid * my_first_scale, axis=0)
    my_grad_input = (
        my_grad_hidden
        + my_first_scale * gained_one
        - my_resid * my_first_scale**3 * jnp.mean(gained_one * my_resid, axis=-1, keepdims=True)
    )
    grad_input = z_gather(my_grad_input.astype(BF16)).astype(F32)
    grad_norm1 = small_sum(grad_norm1[None], True)[0]

    routed = z_scatter(plane_scatter(out_blocks), axis=1)
    mixed = (piece(hidden, tensor_place, col_width, 1) + routed).astype(BF16)

    width = here * units

    def from_chip(total):
        return total[:, :width] + swap(total[:, width:].astype(BF16), 1).astype(F32)

    def as_experts(total):
        return total.reshape(model_width, here, units).transpose(1, 0, 2)

    grad_gate = as_experts(from_chip(gate_total))
    up_weight_gradient = as_experts(from_chip(up_total))
    grad_down = down_total[:width] + swap(down_total[width:].astype(BF16), 1).astype(F32)
    grad_down = grad_down.reshape(here, units, model_width)
    return (
        mixed,
        grad_input,
        grad_norm1,
        grad_weights[:, :q_width],
        grad_weights[:, q_width : q_width + k_width],
        grad_weights[:, q_width + k_width :],
        grad_output,
        early[experts],
        early[:experts].T,
        grad_gate,
        up_weight_gradient,
        grad_down,
    )


def solution(mesh):
    placed = (
        P("expert", None),
        P(),
        P(None, "tensor"),
        P(None, "tensor"),
        P(None, "tensor"),
        P("tensor", None),
        P(),
        P(),
        P("expert", None, "tensor"),
        P("expert", None, "tensor"),
        P("expert", "tensor", None),
        P("expert", None),
        P("expert", None),
    )
    return jax.shard_map(
        local,
        mesh=mesh,
        in_specs=placed,
        out_specs=(
            P("expert", "tensor"),
            P("expert", None),
            P(),
            P(None, "tensor"),
            P(None, "tensor"),
            P(None, "tensor"),
            P("tensor", None),
            P(),
            P(),
            P("expert", None, "tensor"),
            P("expert", None, "tensor"),
            P("expert", "tensor", None),
        ),
        check_vma=False,
    )
```

time: 1040 us -> 467 us (0.45)
  waiting for transfers between devices: 575 us -> 121 us
  blocking collectives: 138 us -> 0 us
  starting transfers between devices: 6.15 us -> 106 us
  local copies, waits for them, and re-layouts: 136 us -> 51.5 us
  matrix products: 64.9 us -> 128 us
  other arithmetic: 93.1 us -> 49.1 us
  between operations: 15.5 us -> 3.63 us
    all_gather x3 -> x0, waiting for transfers between devices: 184 us -> none  [the longest x1 75.3 us: local(): lax.all_gather(expert_up_weight, 'tensor', axis=2, tiled=True)]
    psum x4 -> x0, waiting for transfers between devices: 181 us -> none  [the longest x1 58.3 us: local(): lax.psum(jnp.dot(attended, w_output, preferred_element_type=jnp.float32),...]
    unnamed x13 -> x0, waiting for transfers between devices: 134 us -> none
    ppermute x0 -> x86, waiting for transfers between devices: none -> 121 us  [the longest x56 79.2 us: swap(): return lax.ppermute(array, 'expert', [(i, i ^ mask) for i in range(size)])]
    all_to_all x3 -> x0, blocking collectives: 108 us -> none  [the longest x1 36.6 us: local(): lax.all_to_all(grad_send, 'expert', split_axis=0, concat_axis=1, tiled=True)]
    ppermute x0 -> x86, starting transfers between devices: none -> 106 us  [the longest x30 55.7 us: z_shift(): lax.ppermute(array, 'tensor', [(i, (i + step) % size) for i in range(size)])]
    reduce_scatter x2 -> x0, waiting for transfers between devices: 75.4 us -> none  [the longest x1 75.4 us: local(): lax.psum_scatter(down_total.astype(jnp.bfloat16), 'tensor', scatter_dimen...]
    dot_general x24 -> x55, matrix products: 58.9 us -> 122 us  [the longest x23 47.9 us: mm(): return jnp.dot(left, right, preferred_element_type=F32)]
  transfers between devices with their start and end apart: 12 -> 86, of which waited for: 10 -> 29; matrix products, arithmetic and copies ran while one was open for 20% -> 42% of each run, Pallas kernels for 0% -> 0%
where the time goes in v1:
time: 467 us; the launch traced here: 459 us
  matrix products  128 us (27%)
  waiting for transfers between devices  121 us (26%)
  starting transfers between devices  106 us (23%)
  local copies, waits for them, and re-layouts  51.5 us (11%)
  other arithmetic  49.1 us (11%)
    ppermute x56, waiting for transfers between devices, swap(): return lax.ppermute(array, 'expert', [(i, i ^ mask) for i in range(size)])  79.2 us
    ppermute x30, starting transfers between devices, z_shift(): lax.ppermute(array, 'tensor', [(i, (i + step) % size) for i in range(size)])  55.7 us
    ppermute x56, starting transfers between devices, swap(): return lax.ppermute(array, 'expert', [(i, i ^ mask) for i in range(size)])  50.3 us
    dot_general x23, matrix products, mm(): return jnp.dot(left, right, preferred_element_type=F32)  47.9 us
    ppermute x30, waiting for transfers between devices, z_shift(): lax.ppermute(array, 'tensor', [(i, (i + step) % size) for i in range(size)])  41.8 us
    dot_general x14, matrix products, mm_rows(): lax.dot_general(left, right, (((0,), (0,)), ((), ())), preferred_element_...  41.2 us
    dot_general x16, matrix products, mm_cols(): lax.dot_general(left, right, (((1,), (1,)), ((), ())), preferred_element_...  31.9 us
    unnamed x232, local copies, waits for them, and re-layouts  24.6 us
  transfers between devices with their start and end apart: 86, of which 29 were waited for; matrix products, arithmetic and copies ran while one was open for 42% of the time, Pallas kernels for 0%

profile of v1, /device:TPU:0, one launch (start us, length us, event | category | flops | bytes accessed | tf_op | source)
XLA Modules:
  0.0 459.1 jit_solution(11685623724903805736)
XLA Ops:
  36.8 7.3 %collective-permute-done.19 = s32[4,512]{1,0:T(4,128)S(1)} collective-permute-done((s32[4,512]{1,0:T(4,128)S(1)}, s32[4,512]{1,0:T(4,128)S(1)}, u32[]{:S(2)}, u32[]{:S(2)}) %collective-permute-start.19) | collective-permute-done | bytes 8224 | tf_op jit(solution)/shard_map/ppermute | solution.py:96
  50.1 3.5 collective-permute-done.7
  84.3 3.8 fusion.103
  88.1 3.8 fusion.107
  92.0 19.7 %collective-permute-done.30 = bf16[256,1024]{1,0:T(8,128)(2,1)S(1)} collective-permute-done((bf16[256,1024]{1,0:T(8,128)(2,1)S(1)}, bf16[256,1024]{1,0:T(8,128)(2,1)S(1)}, u32[]{:S(2)}, u32[]{:S(2)}) %collective-permute-start.30) | collective-permute-done | bytes 524320 | tf_op jit(solution)/shard_map/ppermute | solution.py:96
  116.3 3.8 fusion.96
  121.9 6.7 %multiply_convert_fusion.5 = (bf16[512,1024]{1,0:T(8,128)(2,1)}, bf16[512,1024]{1,0:T(8,128)(2,1)}, f32[64,8,8,128]{3,1,2,0:T(8,128)S(1)}, bf16[512,1024]{1,0:T(8,128)(2,1)}) fusion(f32[512,1024]{1,0:T(8,128)} %fusion.96, f32[64,8,8,128]{3,2,1,0:T(8,128)S(1)} %bitcast.326, f32[1024,512]{0,1:T(8,128)} %fusion.103, ...), kind=kOutput, calls=%fused_computation.53 | convolution fusion | flops 1083179008 | bytes 14680064 | tf_op jit(solution)/shard_map/dot_general | solution.py:79
  145.1 4.6 fusion.119
  149.7 4.8 %fusion.116 = f32[1024,1024]{0,1:T(8,128)} fusion(bf16[512,1024]{1,0:T(8,128)(2,1)} %collective-permute-done.14, bf16[512,1024]{1,0:T(8,128)(2,1)S(1)} %copy-done.74), kind=kOutput, calls=%fused_computation.307 | convolution fusion | flops 1073741824 | bytes 6291456 | tf_op jit(solution)/shard_map/dot_general | solution.py:83
  154.5 4.6 fusion.113
  167.1 6.4 %multiply_convert_fusion.1 = (bf16[512,1024]{1,0:T(8,128)(2,1)}, bf16[512,1024]{1,0:T(8,128)(2,1)}, f32[64,8,8,128]{3,1,2,0:T(8,128)S(1)}, bf16[512,1024]{1,0:T(8,128)(2,1)}) fusion(f32[512,1024]{1,0:T(8,128)} %fusion.99, f32[64,8,8,128]{3,2,1,0:T(8,128)S(1)} %bitcast.327, f32[1024,512]{0,1:T(8,128)} %fusion.107, ...), kind=kOutput, calls=%fused_computation.48 | convolution fusion | flops 1083179008 | bytes 14680064 | tf_op jit(solution)/shard_map/dot_general | solution.py:79
  182.9 6.9 %multiply_convert_fusion.3 = (bf16[512,1024]{1,0:T(8,128)(2,1)}, bf16[512,1024]{1,0:T(8,128)(2,1)}, f32[64,8,8,128]{3,1,2,0:T(8,128)S(1)}, bf16[512,1024]{1,0:T(8,128)(2,1)}) fusion(f32[512,1024]{1,0:T(8,128)} %fusion.98, f32[512,1024]{1,0:T(8,128)} %fusion.105, f32[64,8,8,128]{3,2,1,0:T(8,128)S(1)} %bitcast.328, bf16[512,1024]{1,0:T(8,128)(2,1)S(1)} %copy-done.12, ...), kind=kOutput, calls=%fused_computation.51 | convolution fusion | flops 1083179008 | bytes 14680064 | tf_op jit(solution)/shard_map/dot_general | solution.py:79
  208.6 5.3 %fusion.120 = f32[1024,1024]{1,0:T(8,128)} fusion(bf16[512,1024]{1,0:T(8,128)(2,1)S(1)} %copy-done.54, bf16[512,1024]{1,0:T(8,128)(2,1)} %collective-permute-done.31), kind=kOutput, calls=%fused_computation.311 | convolution fusion | flops 1073741824 | bytes 6291456 | tf_op jit(solution)/shard_map/dot_general | solution.py:83
  213.9 3.4 fusion.117
  235.4 4.0 multiply_convert_fusion.7
  282.7 3.8 slice_add_fusion
  286.5 6.1 %collective-permute-done.34 = bf16[512,1024]{1,0:T(8,128)(2,1)} collective-permute-done((bf16[512,1024]{1,0:T(8,128)(2,1)}, bf16[512,1024]{1,0:T(8,128)(2,1)}, u32[]{:S(2)}, u32[]{:S(2)}) %collective-permute-start.34) | collective-permute-done | bytes 1048608 | tf_op jit(solution)/shard_map/ppermute | solution.py:96
  302.9 11.4 %collective-permute-done.23 = bf16[512,1024]{1,0:T(8,128)(2,1)} collective-permute-done((bf16[512,1024]{1,0:T(8,128)(2,1)}, bf16[512,1024]{1,0:T(8,128)(2,1)}, u32[]{:S(2)}, u32[]{:S(2)}) %collective-permute-start.23) | collective-permute-done | bytes 1048608 | tf_op jit(solution)/shard_map/ppermute | solution.py:96
  332.6 17.5 %collective-permute-done.27 = bf16[512,256]{1,0:T(8,128)(2,1)S(1)} collective-permute-done((bf16[512,256]{1,0:T(8,128)(2,1)S(1)}, bf16[512,256]{1,0:T(8,128)(2,1)S(1)}, u32[]{:S(2)}, u32[]{:S(2)}) %collective-permute-start.27) | collective-permute-done | bytes 262176 | tf_op jit(solution)/shard_map/ppermute | solution.py:101
  352.5 10.7 %collective-permute-done.47 = bf16[128,1024]{1,0:T(8,128)(2,1)S(1)} collective-permute-done((bf16[128,1024]{1,0:T(8,128)(2,1)S(1)}, bf16[128,1024]{1,0:T(8,128)(2,1)S(1)}, u32[]{:S(2)}, u32[]{:S(2)}) %collective-permute-start.47) | collective-permute-done | bytes 262176 | tf_op jit(solution)/shard_map/ppermute | solution.py:101
  372.9 5.6 %collective-permute-start.49 = (bf16[128,1024]{1,0:T(8,128)(2,1)S(1)}, bf16[128,1024]{1,0:T(8,128)(2,1)S(1)}, u32[]{:S(2)}, u32[]{:S(2)}) collective-permute-start(bf16[128,1024]{1,0:T(8,128)(2,1)S(1)} %get-tuple-element.50), channel_id=1, source_target_pairs={{0,1},{1,2},{2,3},{3,0},{4,5},{5,6},{6,7},{7,4},{8,9},{9,10},{10,1... | collective-permute-start | bytes 786440 | tf_op jit(solution)/shard_map/ppermute | solution.py:101
  382.8 4.1 collective-permute-done.79
  387.8 8.8 %collective-permute-done.50 = bf16[128,1024]{1,0:T(8,128)(2,1)S(1)} collective-permute-done((bf16[128,1024]{1,0:T(8,128)(2,1)S(1)}, bf16[128,1024]{1,0:T(8,128)(2,1)S(1)}, u32[]{:S(2)}, u32[]{:S(2)}) %collective-permute-start.50) | collective-permute-done | bytes 262176 | tf_op jit(solution)/shard_map/ppermute | solution.py:101
  398.2 11.9 %collective-permute-start.82 = (f32[33,1024]{1,0:T(8,128)S(1)}, f32[33,1024]{1,0:T(8,128)S(1)}, u32[]{:S(2)}, u32[]{:S(2)}) collective-permute-start(f32[33,1024]{1,0:T(8,128)S(1)} %add.622), channel_id=1, source_target_pairs={{0,3},{1,0},{2,1},{3,2},{4,7},{5,4},{6,5},{7,6},{8,11},{9,8},{10,9... | collective-permute-start | bytes 405512 | tf_op jit(solution)/shard_map/ppermute | solution.py:101
  (603 shorter events, 287.2 us)
Async XLA Ops:
  1.7 27.3 %collective-permute-start.1 = (bf16[32,1024]{1,0:T(8,128)(2,1)S(1)}, bf16[32,1024]{1,0:T(8,128)(2,1)S(1)}, u32[]{:S(2)}, u32[]{:S(2)}) collective-permute-start(bf16[32,1024]{1,0:T(8,128)(2,1)S(1)} %constant_dynamic-slice_fusion.10), channel_id=1, source_target_pairs={{0,1},{1,2},{2,3},{3,0},{4,5},{5,6},{6,7},{7,4},{8,9},{9,10},{10,1... | collective-permute-start | bytes 196616 | tf_op jit(solution)/shard_map/ppermute | solution.py:101
  19.5 37.1 %collective-permute-start = (bf16[512,256]{0,1:T(8,128)(2,1)S(1)}, bf16[512,256]{0,1:T(8,128)(2,1)S(1)}, u32[]{:S(2)}, u32[]{:S(2)}) collective-permute-start(bf16[512,256]{0,1:T(8,128)(2,1)S(1)} %bitcast.359), channel_id=1, source_target_pairs={{0,1},{1,2},{2,3},{3,0},{4,5},{5,6},{6,7},{7,4},{8,9},{9,10},{10,1... | collective-permute-start | bytes 786440 | tf_op jit(solution)/shard_map/ppermute | solution.py:101
  62.5 52.0 %collective-permute-start.14 = (bf16[512,1024]{1,0:T(8,128)(2,1)S(1)}, bf16[512,1024]{1,0:T(8,128)(2,1)}, u32[]{:S(2)}, u32[]{:S(2)}) collective-permute-start(bf16[512,1024]{1,0:T(8,128)(2,1)S(1)} %multiply_convert_fusion.8), channel_id=1, source_target_pairs={{0,8},{4,12},{8,0},{12,4},{16,24},{20,28},{24,16},{28,20},{1,9},{5... | collective-permute-start | bytes 3145736 | tf_op jit(solution)/shard_map/ppermute | solution.py:96
  64.2 71.8 %collective-permute-start.17 = (bf16[512,1024]{1,0:T(8,128)(2,1)S(1)}, bf16[512,1024]{1,0:T(8,128)(2,1)S(1)}, u32[]{:S(2)}, u32[]{:S(2)}) collective-permute-start(bf16[512,1024]{1,0:T(8,128)(2,1)S(1)} %multiply_convert_fusion.8), channel_id=1, source_target_pairs={{0,16},{4,20},{8,24},{12,28},{16,0},{20,4},{24,8},{28,12},{1,17},{... | collective-permute-start | bytes 3145736 | tf_op jit(solution)/shard_map/ppermute | solution.py:96
  81.1 30.6 %collective-permute-start.30 = (bf16[256,1024]{1,0:T(8,128)(2,1)S(1)}, bf16[256,1024]{1,0:T(8,128)(2,1)S(1)}, u32[]{:S(2)}, u32[]{:S(2)}) collective-permute-start(bf16[256,1024]{1,0:T(8,128)(2,1)S(1)} %slice.228), channel_id=1, source_target_pairs={{0,16},{4,20},{8,24},{12,28},{16,0},{20,4},{24,8},{28,12},{1,17},{... | collective-permute-start | bytes 1572872 | tf_op jit(solution)/shard_map/ppermute | solution.py:96
  82.7 29.0 %collective-permute-start.32 = (bf16[256,1024]{1,0:T(8,128)(2,1)S(1)}, bf16[256,1024]{1,0:T(8,128)(2,1)S(1)}, u32[]{:S(2)}, u32[]{:S(2)}) collective-permute-start(bf16[256,1024]{1,0:T(8,128)(2,1)S(1)} %slice.229), channel_id=1, source_target_pairs={{0,8},{4,12},{8,0},{12,4},{16,24},{20,28},{24,16},{28,20},{1,9},{5... | collective-permute-start | bytes 1572872 | tf_op jit(solution)/shard_map/ppermute | solution.py:96
  132.6 27.4 %collective-permute-start.40 = (f32[8,512]{1,0:T(8,128)S(1)}, f32[8,512]{1,0:T(8,128)S(1)}, u32[]{:S(2)}, u32[]{:S(2)}) collective-permute-start(f32[8,512]{1,0:T(8,128)S(1)} %bitcast.394), channel_id=1, source_target_pairs={{0,8},{4,12},{8,0},{12,4},{16,24},{20,28},{24,16},{28,20},{1,9},{5... | collective-permute-start | bytes 49160 | tf_op jit(solution)/shard_map/ppermute | solution.py:96
  178.1 43.7 %collective-permute-start.41 = (f32[8,512]{1,0:T(8,128)}, f32[8,512]{1,0:T(8,128)}, u32[]{:S(2)}, u32[]{:S(2)}) collective-permute-start(f32[8,512]{1,0:T(8,128)} %bitcast.392), channel_id=1, source_target_pairs={{0,16},{4,20},{8,24},{12,28},{16,0},{20,4},{24,8},{28,12},{1,17},{... | collective-permute-start | bytes 49160 | tf_op jit(solution)/shard_map/ppermute | solution.py:96
  194.6 28.8 %collective-permute-start.42 = (f32[8,512]{1,0:T(8,128)}, f32[8,512]{1,0:T(8,128)S(1)}, u32[]{:S(2)}, u32[]{:S(2)}) collective-permute-start(f32[8,512]{1,0:T(8,128)} %bitcast.393), channel_id=1, source_target_pairs={{0,24},{4,28},{8,16},{12,20},{16,8},{20,12},{24,0},{28,4},{1,25},{... | collective-permute-start | bytes 49160 | tf_op jit(solution)/shard_map/ppermute | solution.py:96
  202.2 59.8 %collective-permute-start.33 = (bf16[256,1024]{1,0:T(8,128)(2,1)}, bf16[256,1024]{1,0:T(8,128)(2,1)}, u32[]{:S(2)}, u32[]{:S(2)}) collective-permute-start(bf16[256,1024]{1,0:T(8,128)(2,1)} %get-tuple-element.64), channel_id=1, source_target_pairs={{0,16},{4,20},{8,24},{12,28},{16,0},{20,4},{24,8},{28,12},{1,17},{... | collective-permute-start | bytes 1572872 | tf_op jit(solution)/shard_map/ppermute | solution.py:96
  202.7 60.7 %collective-permute-start.35 = (bf16[256,1024]{1,0:T(8,128)(2,1)}, bf16[256,1024]{1,0:T(8,128)(2,1)}, u32[]{:S(2)}, u32[]{:S(2)}) collective-permute-start(bf16[256,1024]{1,0:T(8,128)(2,1)} %get-tuple-element.65), channel_id=1, source_target_pairs={{0,8},{4,12},{8,0},{12,4},{16,24},{20,28},{24,16},{28,20},{1,9},{5... | collective-permute-start | bytes 1572872 | tf_op jit(solution)/shard_map/ppermute | solution.py:96
  229.6 36.7 %collective-permute-start.22 = (bf16[256,1024]{1,0:T(8,128)(2,1)}, bf16[256,1024]{1,0:T(8,128)(2,1)}, u32[]{:S(2)}, u32[]{:S(2)}) collective-permute-start(bf16[256,1024]{1,0:T(8,128)(2,1)} %get-tuple-element.66), channel_id=1, source_target_pairs={{0,16},{4,20},{8,24},{12,28},{16,0},{20,4},{24,8},{28,12},{1,17},{... | collective-permute-start | bytes 1572872 | tf_op jit(solution)/shard_map/ppermute | solution.py:96
  230.5 38.9 %collective-permute-start.24 = (bf16[256,1024]{1,0:T(8,128)(2,1)}, bf16[256,1024]{1,0:T(8,128)(2,1)}, u32[]{:S(2)}, u32[]{:S(2)}) collective-permute-start(bf16[256,1024]{1,0:T(8,128)(2,1)} %get-tuple-element.67), channel_id=1, source_target_pairs={{0,8},{4,12},{8,0},{12,4},{16,24},{20,28},{24,16},{28,20},{1,9},{5... | collective-permute-start | bytes 1572872 | tf_op jit(solution)/shard_map/ppermute | solution.py:96
  246.2 36.6 %collective-permute-start.85 = (bf16[512,1024]{1,0:T(8,128)(2,1)}, bf16[512,1024]{1,0:T(8,128)(2,1)}, u32[]{:S(2)}, u32[]{:S(2)}) collective-permute-start(bf16[512,1024]{1,0:T(8,128)(2,1)} %slice.312), channel_id=1, source_target_pairs={{0,4},{4,0},{8,12},{12,8},{16,20},{20,16},{24,28},{28,24},{1,5},{5... | collective-permute-start | bytes 3145736 | tf_op jit(solution)/shard_map/ppermute | solution.py:96
  273.9 40.4 %collective-permute-start.23 = (bf16[512,1024]{1,0:T(8,128)(2,1)}, bf16[512,1024]{1,0:T(8,128)(2,1)}, u32[]{:S(2)}, u32[]{:S(2)}) collective-permute-start(bf16[512,1024]{1,0:T(8,128)(2,1)} %pad_maximum_fusion.3), channel_id=1, source_target_pairs={{0,8},{4,12},{8,0},{12,4},{16,24},{20,28},{24,16},{28,20},{1,9},{5... | collective-permute-start | bytes 3145736 | tf_op jit(solution)/shard_map/ppermute | solution.py:96
  275.2 42.0 %collective-permute-start.25 = (bf16[512,1024]{1,0:T(8,128)(2,1)}, bf16[512,1024]{1,0:T(8,128)(2,1)}, u32[]{:S(2)}, u32[]{:S(2)}) collective-permute-start(bf16[512,1024]{1,0:T(8,128)(2,1)} %pad_maximum_fusion.4), channel_id=1, source_target_pairs={{0,16},{4,20},{8,24},{12,28},{16,0},{20,4},{24,8},{28,12},{1,17},{... | collective-permute-start | bytes 3145736 | tf_op jit(solution)/shard_map/ppermute | solution.py:96
  320.7 29.4 %collective-permute-start.27 = (bf16[512,256]{1,0:T(8,128)(2,1)S(1)}, bf16[512,256]{1,0:T(8,128)(2,1)S(1)}, u32[]{:S(2)}, u32[]{:S(2)}) collective-permute-start(bf16[512,256]{1,0:T(8,128)(2,1)S(1)} %get-tuple-element.58), channel_id=1, source_target_pairs={{0,2},{1,3},{2,0},{3,1},{4,6},{5,7},{6,4},{7,5},{8,10},{9,11},{10,... | collective-permute-start | bytes 786440 | tf_op jit(solution)/shard_map/ppermute | solution.py:101
  323.1 27.0 %collective-permute-start.28 = (bf16[512,256]{1,0:T(8,128)(2,1)S(1)}, bf16[512,256]{1,0:T(8,128)(2,1)S(1)}, u32[]{:S(2)}, u32[]{:S(2)}) collective-permute-start(bf16[512,256]{1,0:T(8,128)(2,1)S(1)} %get-tuple-element.57), channel_id=1, source_target_pairs={{0,3},{1,0},{2,1},{3,2},{4,7},{5,4},{6,5},{7,6},{8,11},{9,8},{10,9... | collective-permute-start | bytes 786440 | tf_op jit(solution)/shard_map/ppermute | solution.py:101
  327.3 35.9 %collective-permute-start.47 = (bf16[128,1024]{1,0:T(8,128)(2,1)S(1)}, bf16[128,1024]{1,0:T(8,128)(2,1)S(1)}, u32[]{:S(2)}, u32[]{:S(2)}) collective-permute-start(bf16[128,1024]{1,0:T(8,128)(2,1)S(1)} %get-tuple-element.26), channel_id=1, source_target_pairs={{0,2},{1,3},{2,0},{3,1},{4,6},{5,7},{6,4},{7,5},{8,10},{9,11},{10,... | collective-permute-start | bytes 786440 | tf_op jit(solution)/shard_map/ppermute | solution.py:101
  331.3 31.9 %collective-permute-start.48 = (bf16[128,1024]{1,0:T(8,128)(2,1)S(1)}, bf16[128,1024]{1,0:T(8,128)(2,1)S(1)}, u32[]{:S(2)}, u32[]{:S(2)}) collective-permute-start(bf16[128,1024]{1,0:T(8,128)(2,1)S(1)} %get-tuple-element.26), channel_id=1, source_target_pairs={{0,3},{1,0},{2,1},{3,2},{4,7},{5,4},{6,5},{7,6},{8,11},{9,8},{10,9... | collective-permute-start | bytes 786440 | tf_op jit(solution)/shard_map/ppermute | solution.py:101
  351.5 30.0 %collective-permute-start.78 = (f32[33,1024]{1,0:T(8,128)S(1)}, f32[33,1024]{1,0:T(8,128)S(1)}, u32[]{:S(2)}, u32[]{:S(2)}) collective-permute-start(f32[33,1024]{1,0:T(8,128)S(1)} %fusion.82), channel_id=1, source_target_pairs={{0,8},{4,12},{8,0},{12,4},{16,24},{20,28},{24,16},{28,20},{1,9},{5... | collective-permute-start | bytes 405512 | tf_op jit(solution)/shard_map/ppermute | solution.py:96
  382.6 27.5 %collective-permute-start.69 = (bf16[128,1024]{1,0:T(8,128)(2,1)S(1)}, bf16[128,1024]{1,0:T(8,128)(2,1)S(1)}, u32[]{:S(2)}, u32[]{:S(2)}) collective-permute-start(bf16[128,1024]{1,0:T(8,128)(2,1)S(1)} %dynamic-slice_convert_fusion.1), channel_id=1, source_target_pairs={{0,4},{4,0},{8,12},{12,8},{16,20},{20,16},{24,28},{28,24},{1,5},{5... | collective-permute-start | bytes 786440 | tf_op jit(solution)/shard_map/ppermute | solution.py:96
  386.9 46.3 %collective-permute-start.61 = (bf16[512,512]{1,0:T(8,128)(2,1)S(1)}, bf16[512,512]{1,0:T(8,128)(2,1)S(1)}, u32[]{:S(2)}, u32[]{:S(2)}) collective-permute-start(bf16[512,512]{1,0:T(8,128)(2,1)S(1)} %dynamic-slice_convert_fusion), channel_id=1, source_target_pairs={{0,4},{4,0},{8,12},{12,8},{16,20},{20,16},{24,28},{28,24},{1,5},{5... | collective-permute-start | bytes 1572872 | tf_op jit(solution)/shard_map/ppermute | solution.py:96
  386.9 31.4 %collective-permute-start.80 = (f32[33,1024]{1,0:T(8,128)S(1)}, f32[33,1024]{1,0:T(8,128)S(1)}, u32[]{:S(2)}, u32[]{:S(2)}) collective-permute-start(f32[33,1024]{1,0:T(8,128)S(1)} %add.622), channel_id=1, source_target_pairs={{0,1},{1,2},{2,3},{3,0},{4,5},{5,6},{6,7},{7,4},{8,9},{9,10},{10,1... | collective-permute-start | bytes 405512 | tf_op jit(solution)/shard_map/ppermute | solution.py:101
  (174 other events, 1471.9 us)

commit v2 on v1

--- a/solution.py
+++ b/solution.py
@@ -1,8 +1,11 @@
+import functools
 import math
 
 import jax
 import jax.numpy as jnp
 from jax import lax
+from jax.experimental import pallas as pl
+from jax.experimental.pallas import tpu as pltpu
 from jax.sharding import PartitionSpec as P
 
 HEAD_DIMENSION = 64
@@ -15,6 +18,8 @@
 F32 = jnp.float32
 BF16 = jnp.bfloat16
 EXACT = lax.Precision.HIGHEST
+LANES = 128
+TILE = 256
 
 
 def tables(tok_count):
@@ -202,6 +207,129 @@
     return array
 
 
+def expert_kernel(
+    experts,
+    top_count,
+    units,
+    names_ref,
+    normed_ref,
+    grad_ref,
+    router_ref,
+    gate_ref,
+    up_ref,
+    down_ref,
+    out_ref,
+    rows_ref,
+    gate_grad_ref,
+    up_grad_ref,
+    inner_ref,
+):
+    tile, model_width = normed_ref.shape
+    width = gate_ref.shape[1]
+    normed = normed_ref[...]
+    grad = grad_ref[:, :model_width]
+    chosen_names = grad_ref[:, model_width:].astype(F32)
+    lane = lax.broadcasted_iota(jnp.int32, (tile, LANES), 1)
+    lane_float = lane.astype(F32)
+    chosen = lane_float == chosen_names[:, 0:1]
+    for k in range(1, top_count):
+        chosen = chosen | (lane_float == chosen_names[:, k : k + 1])
+    logits = jnp.where(chosen, mm(normed, router_ref[...]), NEGATIVE)
+    expanded = jnp.exp(logits - jnp.max(logits, axis=-1, keepdims=True))
+    expanded = jnp.where(chosen, expanded, 0.0)
+    routing = expanded / jnp.sum(expanded, axis=-1, keepdims=True)
+    grad_routing = jnp.zeros((tile, LANES), F32)
+    columns = min(TILE, width)
+    for start in range(0, width, columns):
+        part = slice(start, start + columns)
+        gate_act = mm(normed, gate_ref[:, part])
+        up_act = mm(normed, up_ref[:, part])
+        grad_plain = mm_cols(grad, down_ref[part, :])
+        weights = []
+        for e in range(start // units, (start + columns) // units):
+            weight = jnp.sum(
+                jnp.where(lane == names_ref[e], routing, 0.0), axis=-1, keepdims=True
+            )
+            weights.append(jnp.broadcast_to(weight, (tile, units)))
+        wide = jnp.concatenate(weights, axis=1) if len(weights) > 1 else weights[0]
+        sigmoid_gate = jax.nn.sigmoid(gate_act)
+        swish = gate_act * sigmoid_gate
+        inner = swish * up_act
+        inner_grad = inner * grad_plain
+        for i, e in enumerate(range(start // units, (start + columns) // units)):
+            total = jnp.sum(inner_grad[:, i * units : (i + 1) * units], axis=-1, keepdims=True)
+            grad_routing = jnp.where(lane == names_ref[e], total, grad_routing)
+        grad_inner = grad_plain * wide
+        inner_ref[:, part] = (inner * wide).astype(BF16)
+        up_grad_ref[:, part] = (grad_inner * swish).astype(BF16)
+        gate_grad_ref[:, part] = (
+            grad_inner * up_act * (sigmoid_gate + swish * (1.0 - sigmoid_gate))
+        ).astype(BF16)
+    rounded = grad_routing.astype(BF16).astype(F32)
+    left = pltpu.roll(grad_routing - rounded, experts, 1)
+    rows_ref[:, model_width:] = (rounded + left).astype(BF16)
+    rows_ref[:, :model_width] = (
+        mm_cols(gate_grad_ref[...], gate_ref[...]) + mm_cols(up_grad_ref[...], up_ref[...])
+    ).astype(BF16)
+    out_ref[...] = mm(inner_ref[...], down_ref[...]).astype(BF16)
+
+
+def expert_block(names, normed, grad, router, gate_w, up_w, down_w, experts, top_count, units):
+    rows, model_width = normed.shape
+    width = gate_w.shape[1]
+    tile = min(TILE, rows)
+
+    def tiled(columns):
+        return pl.BlockSpec((tile, columns), lambda i, names: (i, 0))
+
+    def fixed(array):
+        return pl.BlockSpec(array.shape, lambda i, names: (0, 0))
+
+    def shaped(columns):
+        return jax.ShapeDtypeStruct((rows, columns), BF16)
+
+    return pl.pallas_call(
+        functools.partial(expert_kernel, experts, top_count, units),
+        grid_spec=pltpu.PrefetchScalarGridSpec(
+            num_scalar_prefetch=1,
+            grid=(rows // tile,),
+            in_specs=[
+                tiled(model_width),
+                tiled(model_width + LANES),
+                fixed(router),
+                fixed(gate_w),
+                fixed(up_w),
+                fixed(down_w),
+            ],
+            out_specs=[
+                tiled(model_width),
+                tiled(model_width + LANES),
+                tiled(width),
+                tiled(width),
+                tiled(width),
+            ],
+        ),
+        out_shape=[
+            shaped(model_width),
+            shaped(model_width + LANES),
+            shaped(width),
+            shaped(width),
+            shaped(width),
+        ],
+        compiler_params=pltpu.CompilerParams(vmem_limit_bytes=44 * 1024 * 1024),
+        cost_estimate=pl.CostEstimate(
+            flops=12 * rows * model_width * width,
+            bytes_accessed=6 * model_width * width + 14 * rows * model_width,
+            transcendentals=rows * width,
+        ),
+        name="experts",
+    )(names, normed, grad, router, gate_w, up_w, down_w)
+
+
+def tied(*arrays):
+    return lax.optimization_barrier(arrays)
+
+
 def norm_scale(field):
     return lax.rsqrt(jnp.mean(field * field, axis=-1, keepdims=True) + EPS)
 
@@ -231,7 +359,7 @@
 ):
     tok_count = tokens.shape[0]
     model_width = tokens.shape[1]
-    experts = w_router.shape[1]
+    experts, top_count = w_router.shape[1], expert_ids.shape[1]
     here, units = expert_gate_weight.shape[0], expert_gate_weight.shape[2]
     heads_query = w_query.shape[1] // HEAD_DIMENSION
     heads_kv = key_projection_weight.shape[1] // HEAD_DIMENSION
@@ -245,12 +373,8 @@
     own_rows = tok_count // tensor_count
     col_width = model_width // tensor_count
 
-    ids_blocks = plane_gather(expert_ids.T) if expert_count == 8 else [
-        lax.all_gather(
-            expert_ids, "expert", axis=0, tiled=True, axis_index_groups=same_core_groups()
-        ).T
-    ]
-    grad_blocks = plane_gather(cotangent)
+    names_wide = jnp.pad(expert_ids.astype(BF16), ((0, 0), (0, LANES - top_count)))
+    grad_blocks = plane_gather(jnp.concatenate([cotangent, names_wide], axis=1))
 
     def chip_weights(weight):
         other = swap(weight, 1)
@@ -303,91 +427,70 @@
     attended = attended.reshape(tok_count, heads_query * HEAD_DIMENSION)
 
     attended_parts = z_received(attended)
+    if expert_count == 8:
+        grad_x, grad_y, *attended_parts = tied(grad_blocks[1], grad_blocks[2], *attended_parts)
+        grad_blocks[1], grad_blocks[2] = grad_x, grad_y
     hidden = resid_in + mm(attended, w_output)
     for step in range(1, tensor_count):
         hidden = hidden + mm(attended_parts[step], w_parts[step - 1])
     second_scale = norm_scale(hidden)
     second_norm = (hidden * second_scale * norm2_gain).astype(BF16)
 
-    names = jnp.arange(experts, dtype=jnp.int32)
-    first_here = expert_place * here
-    first_other = (expert_place ^ 1) * here
-    out_blocks, row_blocks, routing_blocks = [], [], []
+    local_names = jnp.concatenate(
+        [
+            expert_place * here + jnp.arange(here, dtype=jnp.int32),
+            (expert_place ^ 1) * here + jnp.arange(here, dtype=jnp.int32),
+        ]
+    )
+    router_wide = jnp.pad(w_router, ((0, 0), (0, LANES - experts)))
+    if expert_count == 8:
+        second_norm, grad_blocks[3] = tied(second_norm, grad_blocks[3])
+    normed_blocks = plane_gather(second_norm)
+    done = [
+        expert_block(
+            local_names,
+            normed,
+            grad,
+            router_wide,
+            gate_w,
+            up_w,
+            down_w,
+            experts,
+            top_count,
+            units,
+        )
+        for normed, grad in zip(normed_blocks, grad_blocks)
+    ]
+    plane_rows = plane_scatter([block[1].astype(F32) for block in done])
+    plane_rows, *out_blocks = tied(plane_rows, *[block[0] for block in done])
+    out_blocks = [block.astype(F32) for block in out_blocks]
+    held = tied(*[array for block in done for array in block[2:]])
+    done = [held[3 * i : 3 * i + 3] for i in range(len(done))]
     gate_total = up_total = down_total = 0.0
-    for normed, grad, ids in zip(plane_gather(second_norm), grad_blocks, ids_blocks):
-        rows = normed.shape[0]
-        chosen = jnp.any(ids.T[:, :, None] == names[None, None, :], axis=1)
-        routing = route(normed, w_router, chosen)
-        weight = jnp.concatenate(
-            [
-                lax.dynamic_slice_in_dim(routing, first_here, here, 1),
-                lax.dynamic_slice_in_dim(routing, first_other, here, 1),
-            ],
-            axis=1,
-        )
-        wide = jnp.repeat(weight, units, axis=1)
-        gate_act = mm(normed, gate_w)
-        up_act = mm(normed, up_w)
-        grad_plain = mm_cols(grad, down_w)
-        sigmoid_gate = jax.nn.sigmoid(gate_act)
-        swish = gate_act * sigmoid_gate
-        inner = swish * up_act
-        grad_inner = grad_plain * wide
-        routing_blocks.append(
-            jnp.sum((inner * grad_plain).reshape(rows, 2 * here, units), axis=-1)
-        )
-        inner_low = (inner * wide).astype(BF16)
-        gate_grad = (
-            grad_inner * up_act * sigmoid_gate * (1.0 + gate_act * (1.0 - sigmoid_gate))
-        ).astype(BF16)
-        up_grad = (grad_inner * swish).astype(BF16)
-        out_blocks.append(mm(inner_low, down_w))
-        row_blocks.append(mm_cols(gate_grad, gate_w) + mm_cols(up_grad, up_w))
-        gate_total = gate_total + mm_rows(normed, gate_grad)
-        up_total = up_total + mm_rows(normed, up_grad)
-        down_total = down_total + mm_rows(inner_low, grad)
-
-    row_sum = z_scatter(plane_scatter(row_blocks))
-
-    if expert_count == 8:
-        grad_routing = jnp.zeros((experts, tok_count), F32)
-        for mask, block in enumerate(routing_blocks):
-            part = block.T
-            part = swap(part, 2 * mask) if mask else part
-            source = (expert_place ^ (2 * mask)) * here
-            source_other = (expert_place ^ (2 * mask) ^ 1) * here
-            grad_routing = lax.dynamic_update_slice_in_dim(grad_routing, part[:here], source, 0)
-            grad_routing = lax.dynamic_update_slice_in_dim(
-                grad_routing, part[here:], source_other, 0
-            )
-    else:
-        block = routing_blocks[0]
-        spread = jnp.zeros((block.shape[0], experts), F32)
-        spread = lax.dynamic_update_slice_in_dim(spread, block[:, :here], first_here, 1)
-        spread = lax.dynamic_update_slice_in_dim(spread, block[:, here:], first_other, 1)
-        grad_routing = lax.psum_scatter(
-            spread,
-            "expert",
-            scatter_dimension=0,
-            tiled=True,
-            axis_index_groups=same_core_groups(),
-        ).T
-    routing_parts = z_received(grad_routing)
-    grad_routing = routing_parts[0]
-    for part in routing_parts[1:]:
-        grad_routing = grad_routing + part
-    grad_routing = grad_routing.T
-    own_chosen = jnp.any(expert_ids[:, :, None] == names[None, None, :], axis=1)
-    own_routing = route(second_norm, w_router, own_chosen)
-    grad_logits = own_routing * (
-        grad_routing - jnp.sum(own_routing * grad_routing, axis=-1, keepdims=True)
-    )
+    for normed, grad, block in zip(normed_blocks, grad_blocks, done):
+        gate_total = gate_total + mm_rows(normed, block[0])
+        up_total = up_total + mm_rows(normed, block[1])
+        down_total = down_total + mm_rows(block[2], grad[:, :model_width])
+
+    row_sum = z_scatter(plane_rows)
+    my_routing_grad = (
+        row_sum[:, model_width : model_width + experts]
+        + row_sum[:, model_width + experts : model_width + 2 * experts]
+    )
+    row_sum = row_sum[:, :model_width]
 
     def mine(array):
         return piece(array, tensor_place, own_rows)
 
-    my_logits, my_hidden, my_scale = mine(grad_logits), mine(hidden), mine(second_scale)
-    my_normed = mine(second_norm).astype(F32)
+    my_hidden, my_scale = mine(hidden), mine(second_scale)
+    my_normed = mine(second_norm)
+    names = jnp.arange(experts, dtype=jnp.int32)
+    my_chosen = jnp.any(mine(expert_ids)[:, :, None] == names[None, None, :], axis=1)
+    my_routing = route(my_normed, w_router, my_chosen)
+    my_normed = my_normed.astype(F32)
+    my_logits = my_routing * (
+        my_routing_grad - jnp.sum(my_routing * my_routing_grad, axis=-1, keepdims=True)
+    )
     router_float = w_router.astype(F32)
     grad_second = row_sum + jnp.dot(my_logits, router_float.T, precision=EXACT)
     grad_router = lax.dot_general(
@@ -401,7 +504,8 @@
         - my_hidden * my_scale**3 * jnp.mean(gained_two * my_hidden, axis=-1, keepdims=True)
     )
     grad_branch = z_gather(my_grad_hidden.astype(BF16))
-    early = small_sum(jnp.concatenate([grad_router, grad_norm2[None]]), True)
+    early = jnp.concatenate([grad_router, grad_norm2[None]])
+    early = lax.psum(lax.psum(early, "tensor"), "expert")
     grad_output = expert_sum(mm_rows(attended, grad_branch))
 
     grad_heads = mm_cols(grad_branch, w_output).astype(BF16)
@@ -436,7 +540,8 @@
     grad_input = z_gather(my_grad_input.astype(BF16)).astype(F32)
     grad_norm1 = small_sum(grad_norm1[None], True)[0]
 
-    routed = z_scatter(plane_scatter(out_blocks), axis=1)
+    plane_out, _ = tied(plane_scatter(out_blocks), grad_branch)
+    routed = z_scatter(plane_out, axis=1)
     mixed = (piece(hidden, tensor_place, col_width, 1) + routed).astype(BF16)
 
     width = here * units

time: 467 us -> 536 us (1.15)
  waiting for transfers between devices: 121 us -> 232 us
  matrix products: 128 us -> 43.3 us
  Pallas kernels: 0 us -> 51.1 us
  starting transfers between devices: 106 us -> 85 us
  between operations: 3.63 us -> 16.2 us
    psum x0 -> x2, waiting for transfers between devices: none -> 78.4 us  [local(): early = lax.psum(lax.psum(early, 'tensor'), 'expert')]
    pallas_call x0 -> x4, Pallas kernels: none -> 51.1 us  [expert_block(): pl.pallas_call(functools.partial(expert_kernel, experts, top_count, units...]
    dot_general x23 -> x8, matrix products: 47.9 us -> 10.3 us  [mm(): return jnp.dot(left, right, preferred_element_type=F32)]
    dot_general x16 -> x4, matrix products: 31.9 us -> 3.09 us  [mm_cols(): lax.dot_general(left, right, (((1,), (1,)), ((), ())), preferred_element_...]
    ppermute x30 -> x24, waiting for transfers between devices: 41.8 us -> 69.8 us  [z_shift(): lax.ppermute(array, 'tensor', [(i, (i + step) % size) for i in range(size)])]
    dot_general x14, matrix products: 41.2 us -> 21.3 us  [mm_rows(): lax.dot_general(left, right, (((0,), (0,)), ((), ())), preferred_element_...]
    ppermute x30 -> x24, starting transfers between devices: 55.7 us -> 43.3 us  [z_shift(): lax.ppermute(array, 'tensor', [(i, (i + step) % size) for i in range(size)])]
    reduce_sum x5 -> x1, other arithmetic: 10.1 us -> 0.2 us  [local(): jnp.sum(my_routing * my_routing_grad, axis=-1, keepdims=True)]
  transfers between devices with their start and end apart: 86 -> 72, of which waited for: 29 -> 26; matrix products, arithmetic and copies ran while one was open for 42% -> 23% of each run, Pallas kernels for 0% -> 6%
where the time goes in v2:
time: 536 us; the launch traced here: 526 us
  waiting for transfers between devices  232 us (43%)
  starting transfers between devices  85 us (16%)
  local copies, waits for them, and re-layouts  53.3 us (10%)
  Pallas kernels  51.1 us (10%)
  other arithmetic  45.4 us (8%)
  matrix products  43.3 us (8%)
  between operations  16.2 us (3%)
    ppermute x46, waiting for transfers between devices, swap(): return lax.ppermute(array, 'expert', [(i, i ^ mask) for i in range(size)])  83.9 us
    psum x2, waiting for transfers between devices, local(): early = lax.psum(lax.psum(early, 'tensor'), 'expert')  78.4 us
    ppermute x24, waiting for transfers between devices, z_shift(): lax.ppermute(array, 'tensor', [(i, (i + step) % size) for i in range(size)])  69.8 us
    pallas_call x4, Pallas kernels, expert_block(): pl.pallas_call(functools.partial(expert_kernel, experts, top_count, units...  51.1 us
    ppermute x24, starting transfers between devices, z_shift(): lax.ppermute(array, 'tensor', [(i, (i + step) % size) for i in range(size)])  43.3 us
    ppermute x46, starting transfers between devices, swap(): return lax.ppermute(array, 'expert', [(i, i ^ mask) for i in range(size)])  41.6 us
    dot_general x14, matrix products, mm_rows(): lax.dot_general(left, right, (((0,), (0,)), ((), ())), preferred_element_...  21.3 us
    unnamed x168, local copies, waits for them, and re-layouts  15.1 us
  transfers between devices with their start and end apart: 72, of which 26 were waited for; matrix products, arithmetic and copies ran while one was open for 23% of the time, Pallas kernels for 6%

profile of v2, /device:TPU:0, one launch (start us, length us, event | category | flops | bytes accessed | tf_op | source)
XLA Modules:
  0.0 526.4 jit_solution(1368245404154902361)
XLA Ops:
  8.9 5.0 collective-permute-start.7
  39.7 6.4 %collective-permute-done.10 = bf16[3,64,1024]{2,1,0:T(8,128)(2,1)} collective-permute-done((bf16[3,64,1024]{2,1,0:T(8,128)(2,1)}, bf16[3,64,1024]{2,1,0:T(8,128)(2,1)}, u32[]{:S(2)}, u32[]{:S(2)}) %collective-permute-start.10) | collective-permute-done | bytes 393248 | tf_op jit(solution)/shard_map/ppermute | solution.py:101
  49.3 3.6 collective-permute-done.12
  77.5 7.0 %collective-permute-done.3 = bf16[512,256]{0,1:T(8,128)(2,1)S(1)} collective-permute-done((bf16[512,256]{0,1:T(8,128)(2,1)S(1)}, bf16[512,256]{0,1:T(8,128)(2,1)S(1)}, u32[]{:S(2)}, u32[]{:S(2)}) %collective-permute-start.3) | collective-permute-done | bytes 262176 | tf_op jit(solution)/shard_map/ppermute | solution.py:106
  92.5 10.3 %collective-permute-done.14 = bf16[256,1152]{1,0:T(8,128)(2,1)S(1)} collective-permute-done((bf16[256,1152]{1,0:T(8,128)(2,1)S(1)}, bf16[256,1152]{1,0:T(8,128)(2,1)S(1)}, u32[]{:S(2)}, u32[]{:S(2)}) %collective-permute-start.14) | collective-permute-done | bytes 589856 | tf_op jit(solution)/shard_map/ppermute | solution.py:101
  108.0 10.9 %experts.4 = (bf16[512,1024]{1,0:T(8,128)(2,1)S(1)}, bf16[512,1152]{1,0:T(8,128)(2,1)S(1)}, bf16[512,1024]{1,0:T(8,128)(2,1)S(1)}, bf16[512,1024]{1,0:T(8,128)(2,1)S(1)}, bf16[512,1024]{1,0:T(8,128)(2,1)S(1)}) custom-call(s32[8]{0:T(128)S(1)} %pad_add_fusion.names_ref, bf16[512,1024]{1,0:T(8,128)(2,1)S(1)} %multiply_convert_fusion.normed_ref, ...), custom_call_target="tpu_custom_call" | custom-call | flops 6442450944 | bytes 13631488 | tf_op jit(solution)/shard_map/experts/pallas_call | solution.py:291
  122.0 6.8 %collective-permute-done.20.normed_ref = bf16[512,1024]{1,0:T(8,128)(2,1)S(1)} collective-permute-done((bf16[512,1024]{1,0:T(8,128)(2,1)S(1)}, bf16[512,1024]{1,0:T(8,128)(2,1)S(1)}, u32[]{:S(2)}, u32[]{:S(2)}) %collective-permute-start.20) | collective-permute-done | bytes 1048608 | tf_op jit(solution)/shard_map/ppermute | solution.py:101
  128.8 10.4 %experts.7 = (bf16[512,1024]{1,0:T(8,128)(2,1)S(1)}, bf16[512,1152]{1,0:T(8,128)(2,1)S(1)}, bf16[512,1024]{1,0:T(8,128)(2,1)S(1)}, bf16[512,1024]{1,0:T(8,128)(2,1)S(1)}, bf16[512,1024]{1,0:T(8,128)(2,1)S(1)}) custom-call(s32[8]{0:T(128)S(1)} %pad_add_fusion.names_ref, bf16[512,1024]{1,0:T(8,128)(2,1)S(1)} %collective-permute-done.20.normed_ref, ...), custom_call_target="tpu_custom_call" | custom-call | flops 6442450944 | bytes 13631488 | tf_op jit(solution)/shard_map/experts/pallas_call | solution.py:291
  145.5 10.6 %experts.5 = (bf16[512,1024]{1,0:T(8,128)(2,1)S(1)}, bf16[512,1152]{1,0:T(8,128)(2,1)S(1)}, bf16[512,1024]{1,0:T(8,128)(2,1)S(1)}, bf16[512,1024]{1,0:T(8,128)(2,1)S(1)}, bf16[512,1024]{1,0:T(8,128)(2,1)S(1)}) custom-call(s32[8]{0:T(128)S(1)} %pad_add_fusion.names_ref, bf16[512,1024]{1,0:T(8,128)(2,1)S(1)} %collective-permute-done.18.normed_ref, ...), custom_call_target="tpu_custom_call" | custom-call | flops 6442450944 | bytes 13631488 | tf_op jit(solution)/shard_map/experts/pallas_call | solution.py:291
  160.3 19.2 %experts.6 = (bf16[512,1024]{1,0:T(8,128)(2,1)S(1)}, bf16[512,1152]{1,0:T(8,128)(2,1)S(1)}, bf16[512,1024]{1,0:T(8,128)(2,1)S(1)}, bf16[512,1024]{1,0:T(8,128)(2,1)S(1)}, bf16[512,1024]{1,0:T(8,128)(2,1)S(1)}) custom-call(s32[8]{0:T(128)S(1)} %pad_add_fusion.names_ref, bf16[512,1024]{1,0:T(8,128)(2,1)S(1)} %constant_dynamic-update-slice_fusion.21.normed_ref, ...), custom_call_target="tpu_custom_call" | custom-call | flops 6442450944 | bytes 13631488 | tf_op jit(solution)/shard_map/experts/pallas_call | solution.py:291
  214.6 18.3 %collective-permute-done.25 = bf16[512,1152]{1,0:T(8,128)(2,1)S(1)} collective-permute-done((bf16[512,1152]{1,0:T(8,128)(2,1)S(1)}, bf16[512,1152]{1,0:T(8,128)(2,1)S(1)}, u32[]{:S(2)}, u32[]{:S(2)}) %collective-permute-start.25) | collective-permute-done | bytes 1179680 | tf_op jit(solution)/shard_map/ppermute | solution.py:101
  238.5 5.4 %collective-permute-start.31 = (bf16[128,1152]{1,0:T(8,128)(2,1)}, bf16[128,1152]{1,0:T(8,128)(2,1)}, u32[]{:S(2)}, u32[]{:S(2)}) collective-permute-start(bf16[128,1152]{1,0:T(8,128)(2,1)} %get-tuple-element.124), channel_id=1, source_target_pairs={{0,2},{1,3},{2,0},{3,1},{4,6},{5,7},{6,4},{7,5},{8,10},{9,11},{10,... | collective-permute-start | bytes 884744 | tf_op jit(solution)/shard_map/ppermute | solution.py:106
  257.6 11.4 %collective-permute-done.31 = bf16[128,1152]{1,0:T(8,128)(2,1)} collective-permute-done((bf16[128,1152]{1,0:T(8,128)(2,1)}, bf16[128,1152]{1,0:T(8,128)(2,1)}, u32[]{:S(2)}, u32[]{:S(2)}) %collective-permute-start.31) | collective-permute-done | bytes 294944 | tf_op jit(solution)/shard_map/ppermute | solution.py:106
  273.5 32.2 %all-reduce.5.cloned.1.call-done = f32[33,1024]{1,0:T(8,128)} async-done(((f32[33,1024]{1,0:T(8,128)}), f32[33,1024]{1,0:T(8,128)}) %all-reduce.5.cloned.1.call-update) | async-done | bytes 135184 | tf_op jit(solution)/shard_map/psum | solution.py:508
  314.5 46.3 %all-reduce.7.cloned.1.call-done = f32[33,1024]{1,0:T(8,128)} async-done(((f32[33,1024]{1,0:T(8,128)}), f32[33,1024]{1,0:T(8,128)}) %all-reduce.7.cloned.1.call-update) | async-done | bytes 135184 | tf_op jit(solution)/shard_map/psum | solution.py:508
  384.4 3.4 collective-permute-start.41
  390.8 3.8 collective-permute-done.41
  394.6 14.3 %collective-permute-done.40 = bf16[128,1024]{1,0:T(8,128)(2,1)S(1)} collective-permute-done((bf16[128,1024]{1,0:T(8,128)(2,1)S(1)}, bf16[128,1024]{1,0:T(8,128)(2,1)S(1)}, u32[]{:S(2)}, u32[]{:S(2)}) %collective-permute-start.40) | collective-permute-done | bytes 262176 | tf_op jit(solution)/shard_map/ppermute | solution.py:106
  428.7 20.9 %collective-permute-done.63 = bf16[32,1024]{1,0:T(8,128)(2,1)S(1)} collective-permute-done((bf16[32,1024]{1,0:T(8,128)(2,1)S(1)}, bf16[32,1024]{1,0:T(8,128)(2,1)S(1)}, u32[]{:S(2)}, u32[]{:S(2)}) %collective-permute-start.63) | collective-permute-done | bytes 65568 | tf_op jit(solution)/shard_map/ppermute | solution.py:101
  463.5 6.6 %collective-permute-done.42 = bf16[128,1024]{1,0:T(8,128)(2,1)S(1)} collective-permute-done((bf16[128,1024]{1,0:T(8,128)(2,1)S(1)}, bf16[128,1024]{1,0:T(8,128)(2,1)S(1)}, u32[]{:S(2)}, u32[]{:S(2)}) %collective-permute-start.42) | collective-permute-done | bytes 262176 | tf_op jit(solution)/shard_map/ppermute | solution.py:106
  471.1 6.4 %collective-permute-done.43 = bf16[128,1024]{1,0:T(8,128)(2,1)S(1)} collective-permute-done((bf16[128,1024]{1,0:T(8,128)(2,1)S(1)}, bf16[128,1024]{1,0:T(8,128)(2,1)S(1)}, u32[]{:S(2)}, u32[]{:S(2)}) %collective-permute-start.43) | collective-permute-done | bytes 262176 | tf_op jit(solution)/shard_map/ppermute | solution.py:106
  480.3 5.3 %collective-permute-done.56 = bf16[128,512]{1,0:T(8,128)(2,1)S(1)} collective-permute-done((bf16[128,512]{1,0:T(8,128)(2,1)S(1)}, bf16[128,512]{1,0:T(8,128)(2,1)S(1)}, u32[]{:S(2)}, u32[]{:S(2)}) %collective-permute-start.56) | collective-permute-done | bytes 131104 | tf_op jit(solution)/shard_map/ppermute | solution.py:101
  487.0 4.4 collective-permute-start.38
  498.1 16.9 %collective-permute-done.37 = bf16[512,256]{1,0:T(8,128)(2,1)S(1)} collective-permute-done((bf16[512,256]{1,0:T(8,128)(2,1)S(1)}, bf16[512,256]{1,0:T(8,128)(2,1)S(1)}, u32[]{:S(2)}, u32[]{:S(2)}) %collective-permute-start.37) | collective-permute-done | bytes 262176 | tf_op jit(solution)/shard_map/ppermute | solution.py:106
  (452 shorter events, 224.5 us)
Async XLA Ops:
  7.2 298.4 %all-reduce.5.cloned.1.call-start = ((), (), s32[]{:S(2)}) async-start(), calls=%async_computation | async-start | bytes 327680 | tf_op jit(solution)/shard_map/psum | solution.py:508
  14.9 50.3 %collective-permute-start.15 = (bf16[4,1024,128]{2,1,0:T(8,128)(2,1)}, bf16[4,1024,128]{2,1,0:T(8,128)(2,1)}, u32[]{:S(2)}, u32[]{:S(2)}) collective-permute-start(bf16[4,1024,128]{2,1,0:T(8,128)(2,1)} %param.21), channel_id=1, source_target_pairs={{0,4},{4,0},{8,12},{12,8},{16,20},{20,16},{24,28},{28,24},{1,5},{5... | collective-permute-start | bytes 3145736 | tf_op jit(solution)/shard_map/ppermute | solution.py:101
  14.9 54.4 %collective-permute-start.16 = (bf16[4,1024,128]{2,1,0:T(8,128)(2,1)}, bf16[4,1024,128]{2,1,0:T(8,128)(2,1)}, u32[]{:S(2)}, u32[]{:S(2)}) collective-permute-start(bf16[4,1024,128]{2,1,0:T(8,128)(2,1)} %param.22), channel_id=1, source_target_pairs={{0,4},{4,0},{8,12},{12,8},{16,20},{20,16},{24,28},{28,24},{1,5},{5... | collective-permute-start | bytes 3145736 | tf_op jit(solution)/shard_map/ppermute | solution.py:101
  27.2 43.1 %collective-permute-start.17 = (bf16[4,128,1024]{2,1,0:T(8,128)(2,1)}, bf16[4,128,1024]{2,1,0:T(8,128)(2,1)}, u32[]{:S(2)}, u32[]{:S(2)}) collective-permute-start(bf16[4,128,1024]{2,1,0:T(8,128)(2,1)} %param.23), channel_id=1, source_target_pairs={{0,4},{4,0},{8,12},{12,8},{16,20},{20,16},{24,28},{28,24},{1,5},{5... | collective-permute-start | bytes 3145736 | tf_op jit(solution)/shard_map/ppermute | solution.py:101
  52.9 31.5 %collective-permute-start = (bf16[512,1152]{1,0:T(8,128)(2,1)}, bf16[512,1152]{1,0:T(8,128)(2,1)}, u32[]{:S(2)}, u32[]{:S(2)}) collective-permute-start(bf16[512,1152]{1,0:T(8,128)(2,1)} %fusion.14.grad_ref), channel_id=1, source_target_pairs={{0,8},{4,12},{8,0},{12,4},{16,24},{20,28},{24,16},{28,20},{1,9},{5... | collective-permute-start | bytes 3538952 | tf_op jit(solution)/shard_map/ppermute | solution.py:101
  53.6 30.9 %collective-permute-start.1 = (bf16[512,1152]{1,0:T(8,128)(2,1)}, bf16[512,1152]{1,0:T(8,128)(2,1)S(1)}, u32[]{:S(2)}, u32[]{:S(2)}) collective-permute-start(bf16[512,1152]{1,0:T(8,128)(2,1)} %fusion.14.grad_ref), channel_id=1, source_target_pairs={{0,16},{4,20},{8,24},{12,28},{16,0},{20,4},{24,8},{28,12},{1,17},{... | collective-permute-start | bytes 3538952 | tf_op jit(solution)/shard_map/ppermute | solution.py:101
  106.1 36.1 %collective-permute-start.18 = (bf16[512,1024]{1,0:T(8,128)(2,1)S(1)}, bf16[512,1024]{1,0:T(8,128)(2,1)S(1)}, u32[]{:S(2)}, u32[]{:S(2)}) collective-permute-start(bf16[512,1024]{1,0:T(8,128)(2,1)S(1)} %multiply_convert_fusion.normed_ref), channel_id=1, source_target_pairs={{0,8},{4,12},{8,0},{12,4},{16,24},{20,28},{24,16},{28,20},{1,9},{5... | collective-permute-start | bytes 3145736 | tf_op jit(solution)/shard_map/ppermute | solution.py:101
  205.0 27.9 %collective-permute-start.25 = (bf16[512,1152]{1,0:T(8,128)(2,1)S(1)}, bf16[512,1152]{1,0:T(8,128)(2,1)S(1)}, u32[]{:S(2)}, u32[]{:S(2)}) collective-permute-start(bf16[512,1152]{1,0:T(8,128)(2,1)S(1)} %pad_maximum_fusion.3), channel_id=1, source_target_pairs={{0,16},{4,20},{8,24},{12,28},{16,0},{20,4},{24,8},{28,12},{1,17},{... | collective-permute-start | bytes 3538952 | tf_op jit(solution)/shard_map/ppermute | solution.py:101
  206.9 27.8 %collective-permute-start.23 = (bf16[512,1152]{1,0:T(8,128)(2,1)S(1)}, bf16[512,1152]{1,0:T(8,128)(2,1)S(1)}, u32[]{:S(2)}, u32[]{:S(2)}) collective-permute-start(bf16[512,1152]{1,0:T(8,128)(2,1)S(1)} %pad_maximum_fusion.2), channel_id=1, source_target_pairs={{0,8},{4,12},{8,0},{12,4},{16,24},{20,28},{24,16},{28,20},{1,9},{5... | collective-permute-start | bytes 3538952 | tf_op jit(solution)/shard_map/ppermute | solution.py:101
  209.7 34.1 %collective-permute-start.69 = (bf16[512,1024]{1,0:T(8,128)(2,1)S(1)}, bf16[512,1024]{1,0:T(8,128)(2,1)S(1)}, u32[]{:S(2)}, u32[]{:S(2)}) collective-permute-start(bf16[512,1024]{1,0:T(8,128)(2,1)S(1)} %slice.300), channel_id=1, source_target_pairs={{0,4},{4,0},{8,12},{12,8},{16,20},{20,16},{24,28},{28,24},{1,5},{5... | collective-permute-start | bytes 3145736 | tf_op jit(solution)/shard_map/ppermute | solution.py:101
  238.5 30.5 %collective-permute-start.31 = (bf16[128,1152]{1,0:T(8,128)(2,1)}, bf16[128,1152]{1,0:T(8,128)(2,1)}, u32[]{:S(2)}, u32[]{:S(2)}) collective-permute-start(bf16[128,1152]{1,0:T(8,128)(2,1)} %get-tuple-element.124), channel_id=1, source_target_pairs={{0,2},{1,3},{2,0},{3,1},{4,6},{5,7},{6,4},{7,5},{8,10},{9,11},{10,... | collective-permute-start | bytes 884744 | tf_op jit(solution)/shard_map/ppermute | solution.py:106
  243.8 25.1 %collective-permute-start.30 = (bf16[128,1152]{1,0:T(8,128)(2,1)}, bf16[128,1152]{1,0:T(8,128)(2,1)}, u32[]{:S(2)}, u32[]{:S(2)}) collective-permute-start(bf16[128,1152]{1,0:T(8,128)(2,1)} %get-tuple-element.122), channel_id=1, source_target_pairs={{0,1},{1,2},{2,3},{3,0},{4,5},{5,6},{6,7},{7,4},{8,9},{9,10},{10,1... | collective-permute-start | bytes 884744 | tf_op jit(solution)/shard_map/ppermute | solution.py:106
  254.4 109.3 %collective-permute-start.28 = (bf16[256,1024]{1,0:T(8,128)(2,1)}, bf16[256,1024]{1,0:T(8,128)(2,1)}, u32[]{:S(2)}, u32[]{:S(2)}) collective-permute-start(bf16[256,1024]{1,0:T(8,128)(2,1)} %get-tuple-element.139), channel_id=1, source_target_pairs={{0,8},{4,12},{8,0},{12,4},{16,24},{20,28},{24,16},{28,20},{1,9},{5... | collective-permute-start | bytes 1572872 | tf_op jit(solution)/shard_map/ppermute | solution.py:101
  255.3 113.2 %collective-permute-start.26 = (bf16[256,1024]{1,0:T(8,128)(2,1)}, bf16[256,1024]{1,0:T(8,128)(2,1)}, u32[]{:S(2)}, u32[]{:S(2)}) collective-permute-start(bf16[256,1024]{1,0:T(8,128)(2,1)} %get-tuple-element.138), channel_id=1, source_target_pairs={{0,16},{4,20},{8,24},{12,28},{16,0},{20,4},{24,8},{28,12},{1,17},{... | collective-permute-start | bytes 1572872 | tf_op jit(solution)/shard_map/ppermute | solution.py:101
  273.4 87.4 %all-reduce.7.cloned.1.call-start = ((), (), s32[]{:S(2)}) async-start(), calls=%async_computation.1 | async-start | bytes 327680 | tf_op jit(solution)/shard_map/psum | solution.py:508
  309.3 60.5 %collective-permute-start.33 = (bf16[128,1024]{1,0:T(8,128)(2,1)}, bf16[128,1024]{1,0:T(8,128)(2,1)}, u32[]{:S(2)}, u32[]{:S(2)}) collective-permute-start(bf16[128,1024]{1,0:T(8,128)(2,1)} %get-tuple-element.116), channel_id=1, source_target_pairs={{0,1},{1,2},{2,3},{3,0},{4,5},{5,6},{6,7},{7,4},{8,9},{9,10},{10,1... | collective-permute-start | bytes 786440 | tf_op jit(solution)/shard_map/ppermute | solution.py:106
  310.7 61.0 %collective-permute-start.34 = (bf16[128,1024]{1,0:T(8,128)(2,1)}, bf16[128,1024]{1,0:T(8,128)(2,1)}, u32[]{:S(2)}, u32[]{:S(2)}) collective-permute-start(bf16[128,1024]{1,0:T(8,128)(2,1)} %get-tuple-element.116), channel_id=1, source_target_pairs={{0,2},{1,3},{2,0},{3,1},{4,6},{5,7},{6,4},{7,5},{8,10},{9,11},{10,... | collective-permute-start | bytes 786440 | tf_op jit(solution)/shard_map/ppermute | solution.py:106
  312.0 61.3 %collective-permute-start.35 = (bf16[128,1024]{1,0:T(8,128)(2,1)}, bf16[128,1024]{1,0:T(8,128)(2,1)S(1)}, u32[]{:S(2)}, u32[]{:S(2)}) collective-permute-start(bf16[128,1024]{1,0:T(8,128)(2,1)} %get-tuple-element.116), channel_id=1, source_target_pairs={{0,3},{1,0},{2,1},{3,2},{4,7},{5,4},{6,5},{7,6},{8,11},{9,8},{10,9... | collective-permute-start | bytes 786440 | tf_op jit(solution)/shard_map/ppermute | solution.py:106
  366.1 120.1 %collective-permute-start.29 = (bf16[512,1024]{1,0:T(8,128)(2,1)S(1)}, bf16[512,1024]{1,0:T(8,128)(2,1)S(1)}, u32[]{:S(2)}, u32[]{:S(2)}) collective-permute-start(bf16[512,1024]{1,0:T(8,128)(2,1)S(1)} %pad_maximum_fusion.5), channel_id=1, source_target_pairs={{0,16},{4,20},{8,24},{12,28},{16,0},{20,4},{24,8},{28,12},{1,17},{... | collective-permute-start | bytes 3145736 | tf_op jit(solution)/shard_map/ppermute | solution.py:101
  418.5 33.4 %collective-permute-start.51 = (bf16[512,512]{1,0:T(8,128)(2,1)S(1)}, bf16[512,512]{1,0:T(8,128)(2,1)S(1)}, u32[]{:S(2)}, u32[]{:S(2)}) collective-permute-start(bf16[512,512]{1,0:T(8,128)(2,1)S(1)} %dynamic-slice_convert_fusion), channel_id=1, source_target_pairs={{0,4},{4,0},{8,12},{12,8},{16,20},{20,16},{24,28},{28,24},{1,5},{5... | collective-permute-start | bytes 1572872 | tf_op jit(solution)/shard_map/ppermute | solution.py:101
  423.4 62.9 %collective-permute-start.27 = (bf16[512,1024]{1,0:T(8,128)(2,1)S(1)}, bf16[512,1024]{1,0:T(8,128)(2,1)S(1)}, u32[]{:S(2)}, u32[]{:S(2)}) collective-permute-start(bf16[512,1024]{1,0:T(8,128)(2,1)S(1)} %pad_maximum_fusion.4), channel_id=1, source_target_pairs={{0,8},{4,12},{8,0},{12,4},{16,24},{20,28},{24,16},{28,20},{1,9},{5... | collective-permute-start | bytes 3145736 | tf_op jit(solution)/shard_map/ppermute | solution.py:101
  427.3 25.5 %collective-permute-start.64 = (bf16[32,1024]{1,0:T(8,128)(2,1)S(1)}, bf16[32,1024]{1,0:T(8,128)(2,1)S(1)}, u32[]{:S(2)}, u32[]{:S(2)}) collective-permute-start(bf16[32,1024]{1,0:T(8,128)(2,1)S(1)} %get-tuple-element.107), channel_id=1, source_target_pairs={{0,16},{4,20},{8,24},{12,28},{16,0},{20,4},{24,8},{28,12},{1,17},{... | collective-permute-start | bytes 196616 | tf_op jit(solution)/shard_map/ppermute | solution.py:101
  461.9 29.4 %collective-permute-start.44 = (bf16[128,1024]{1,0:T(8,128)(2,1)S(1)}, bf16[128,1024]{1,0:T(8,128)(2,1)S(1)}, u32[]{:S(2)}, u32[]{:S(2)}) collective-permute-start(bf16[128,1024]{1,0:T(8,128)(2,1)S(1)} %get-tuple-element.111), channel_id=1, source_target_pairs={{0,3},{1,0},{2,1},{3,2},{4,7},{5,4},{6,5},{7,6},{8,11},{9,8},{10,9... | collective-permute-start | bytes 786440 | tf_op jit(solution)/shard_map/ppermute | solution.py:106
  485.7 31.2 %collective-permute-start.58 = (bf16[512,512]{1,0:T(8,128)(2,1)S(1)}, bf16[512,512]{1,0:T(8,128)(2,1)S(1)}, u32[]{:S(2)}, u32[]{:S(2)}) collective-permute-start(bf16[512,512]{1,0:T(8,128)(2,1)S(1)} %constant_dynamic-update-slice_fusion.6), channel_id=1, source_target_pairs={{0,4},{4,0},{8,12},{12,8},{16,20},{20,16},{24,28},{28,24},{1,5},{5... | collective-permute-start | bytes 1572872 | tf_op jit(solution)/shard_map/ppermute | solution.py:101
  (131 other events, 1218.7 us)
Sparse Core Ops, SparseCore 0:
  273.6 32.0 all-reduce.4
  309.1 51.6 all-reduce.6
